TPU v7x, 768 devices: a whole 4x8x12 slice. The times are simulated.
768 devices in a mesh: tile: 48 (over x, z), rep: 16 (over y, core).
Axes of the slice: x: 4, y: 8, z: 12, core: 2. Of those that a mesh axis runs over, the one named last changes fastest.
Arguments:
- amplitudes: bfloat16 [144, 960, 960], P('tile', None, 'rep'), may hold values from -6 to 6, as said below
- occ_energy: float32 [12], replicated, may hold values from -3 to -0.5
- vir_energy: float32 [960], replicated, may hold values from 0.5 to 4
- occ_irrep: int32 [12], replicated, may hold values from 0 to 7, as said below
- vir_irrep: int32 [960], replicated, may hold values from 0 to 7, as said below
- factors: bfloat16 [12, 960, 2048], P(None, 'rep'), as said below
Outputs:
- updated: float32 [12, 960, 12, 960], P(None, 'tile', None, 'rep')
Inputs may be any that keep to these rules, and one draw needn't show every extreme that they name: `occ_irrep`: sorted: the occupied orbitals come in contiguous blocks of one irrep each, and every irrep occurs. `vir_irrep`: sorted: the virtual orbitals come in 8 contiguous blocks, one for each irrep. `amplitudes`: zero wherever occ_irrep[i] xor occ_irrep[j] xor vir_irrep[a] xor vir_irrep[b] is not 0. The auxiliary functions come in 8 contiguous blocks of one irrep each; factors[k, c, P] is zero unless occ_irrep[k] xor vir_irrep[c] equals the irrep of P.
All inputs are finite; a program needn't handle non-finite values.
Results may differ from a plain program's by a relative error of at most 0.0015.
Values may be sent and summed in bfloat16 or wider, within the bound.
A program may use at most 32 MiB of HBM per device.

v0:
```python
import jax
import jax.numpy as jnp
from jax import lax
from jax.sharding import PartitionSpec as P


def per_device(amplitudes, occ_energy, vir_energy, occ_irrep, vir_irrep, factors):
    tile_count = lax.axis_size("tile")
    occ_count = occ_energy.shape[0]
    vir_count = vir_energy.shape[0]
    first_width = vir_count // tile_count
    second_width = amplitudes.shape[2]
    relaid = lax.all_to_all(amplitudes, "tile", split_axis=1, concat_axis=0, tiled=True)
    relaid = relaid.reshape(occ_count, occ_count, first_width, second_width).transpose(0, 2, 1, 3)
    matrix = relaid.reshape(occ_count * first_width, occ_count * second_width)
    factor_rows = factors.reshape(occ_count * second_width, factors.shape[2])
    partial_value = jnp.dot(matrix, factor_rows, preferred_element_type=jnp.float32)
    inter = lax.psum(partial_value.astype(jnp.bfloat16), "rep")
    cycle = jnp.einsum("mq,nq->mn", inter, factor_rows, preferred_element_type=jnp.float32)
    cycle = cycle.reshape(occ_count, first_width, occ_count, second_width)
    tile_start = lax.axis_index("tile") * first_width
    rep_start = lax.axis_index("rep") * second_width
    vir_first = lax.dynamic_slice_in_dim(vir_energy, tile_start, first_width)
    vir_second = lax.dynamic_slice_in_dim(vir_energy, rep_start, second_width)
    irrep_first = lax.dynamic_slice_in_dim(vir_irrep, tile_start, first_width)
    irrep_second = lax.dynamic_slice_in_dim(vir_irrep, rep_start, second_width)
    denom = (
        occ_energy[:, None, None, None]
        - vir_first[None, :, None, None]
        + occ_energy[None, None, :, None]
        - vir_second[None, None, None, :]
    )
    symmetry = jnp.bitwise_xor(
        jnp.bitwise_xor(occ_irrep[:, None, None, None], irrep_first[None, :, None, None]),
        jnp.bitwise_xor(occ_irrep[None, None, :, None], irrep_second[None, None, None, :]),
    )
    return jnp.where(symmetry == 0, relaid.astype(jnp.float32) + cycle / denom, jnp.float32(0.0))


def solution(mesh):
    return jax.shard_map(
        per_device,
        mesh=mesh,
        in_specs=(P("tile", None, "rep"), P(), P(), P(), P(), P(None, "rep", None)),
        out_specs=P(None, "tile", None, "rep"),
        check_vma=False,
    )
```

profile of v0, /device:TPU:1, one launch (start us, length us, event | category | flops | bytes accessed | tf_op | source)
XLA Modules:
  0.0 185.7 jit_solution(7388304380259542454)
XLA Ops:
  6.5 2.0 %copy.11 = bf16[3,960,60]{2,0,1:T(4,128)(2,1)S(1)} copy(bf16[3,960,60]{1,2,0:T(8,128)(2,1)} %param.6) | data formatting | bytes 691200 | tf_op args[0]
  8.5 1.9 reshape.123
  10.4 18.8 %all-to-all-start = ((bf16[48,2,1800]{2,1,0:T(2,128)(2,1)}), bf16[48,2,1800]{2,1,0:T(2,128)(2,1)S(1)}, u32[]{:S(2)}, u32[]{:S(2)}) async-start(bf16[48,2,1800]{2,1,0:T(2,128)(2,1)} %reshape.123), calls=%async_computation | async-start | bytes 737280 | tf_op jit(solution)/shard_map/all_to_all | solution.py:13
  29.2 0.0 all-reduce.2.cloned.1.call-start
  29.3 4.5 %reshape.120 = bf16[720,2048]{1,0:T(8,128)(2,1)} reshape(bf16[12,60,2048]{2,1,0:T(8,128)(2,1)} %param.11) | data formatting | bytes 5898240 | tf_op jit(solution)/shard_map/reshape | solution.py:16
  33.8 0.8 dynamic_slice.13
  34.6 0.8 dynamic_slice.12
  35.3 0.1 broadcast_xor_fusion
  35.4 12.3 %all-to-all-done = bf16[48,2,1800]{2,1,0:T(2,128)(2,1)S(1)} async-done(((bf16[48,2,1800]{2,1,0:T(2,128)(2,1)}), bf16[48,2,1800]{2,1,0:T(2,128)(2,1)S(1)}, u32[]{:S(2)}, u32[]{:S(2)}) %all-to-all-start) | async-done | bytes 345632 | tf_op jit(solution)/shard_map/all_to_all | solution.py:13
  47.7 1.0 reshape.124
  48.7 0.2 copy.17
  48.9 0.2 copy.14
  49.1 0.9 reshape.119
  50.0 2.8 %convolution_convert_fusion = bf16[240,2048]{1,0:T(8,128)(2,1)S(1)} fusion(bf16[240,720]{1,0:T(8,128)(2,1)S(1)} %reshape.119, bf16[720,2048]{1,0:T(8,128)(2,1)} %reshape.120), kind=kOutput, calls=%fused_computation.2 | convolution fusion | flops 708280320 | bytes 4277760 | tf_op jit(solution)/shard_map/dot_general | solution.py:17
  52.8 0.0 copy-start
  52.8 1.1 dot_general.9
  53.9 0.0 all-reduce.2.cloned.1.call-update
  53.9 0.1 broadcast_xor_fusion.1
  54.0 0.8 dynamic_slice.15
  54.8 0.8 dynamic_slice.14
  55.5 0.1 broadcast_subtract_fusion
  55.6 0.1 broadcast_add_fusion
  55.7 117.5 %all-reduce.2.cloned.1.call-done = bf16[12,20,2048]{2,1,0:T(8,128)(2,1)} async-done(((bf16[12,20,2048]{2,1,0:T(8,128)(2,1)}), bf16[12,20,2048]{2,1,0:T(8,128)(2,1)}) %all-reduce.2.cloned.1.call-update) | async-done | bytes 983056 | tf_op jit(solution)/shard_map/psum | solution.py:18
  173.2 5.7 %add_select_fusion = f32[12,20,12,60]{3,1,2,0:T(8,128)} fusion(bf16[12,20,12,60]{3,1,2,0:T(8,128)(2,1)S(1)} %bitcast.24, bf16[12,60,2048]{2,1,0:T(8,128)(2,1)} %param.11, bf16[12,20,2048]{2,1,0:T(8,128)(2,1)} %all-reduce.2.cloned.1.call-done, f32[60]{0:T(128)S(1)} %dynamic_slice.15, f32[12,20,12]{1,2,0:T(8,128)S(1)} %broadcast_add_fusion, ...), kind=kOutput, calls=%fused_computation.3 | convolution fusion | flops 708998400 | bytes 4984560 | tf_op jit(solution)/shard_map/mq,nq->mn/dot_general | solution.py:19
  (3 shorter events, 0.0 us)
Async XLA Ops:
  10.4 37.3 %all-to-all-start = ((bf16[48,2,1800]{2,1,0:T(2,128)(2,1)}), bf16[48,2,1800]{2,1,0:T(2,128)(2,1)S(1)}, u32[]{:S(2)}, u32[]{:S(2)}) async-start(bf16[48,2,1800]{2,1,0:T(2,128)(2,1)} %reshape.123), calls=%async_computation | async-start | bytes 737280 | tf_op jit(solution)/shard_map/all_to_all | solution.py:13
  29.2 144.0 %all-reduce.2.cloned.1.call-start = ((), (), s32[]{:S(2)}) async-start(), calls=%async_computation.1 | async-start | bytes 2359296 | tf_op jit(solution)/shard_map/psum | solution.py:18
  29.3 6.1 %copy-start.1 = (s32[12]{0:T(128)S(1)}, s32[12]{0:T(128)}, u32[]{:S(2)}) copy-start(s32[12]{0:T(128)} %param.9) | copy-start | bytes 148
  52.8 2.8 %copy-start = (f32[12]{0:T(128)S(1)}, f32[12]{0:T(128)}, u32[]{:S(2)}) copy-start(f32[12]{0:T(128)} %param.7) | copy-start | bytes 148
Sparse Core Ops, SparseCore 0:
  54.1 119.1 all-reduce.1
where the time goes:
time: 186 us
  waiting for transfers between devices  130 us (70%)
  starting transfers between devices  18.9 us (10%)
  local copies, waits for them, and re-layouts  14.8 us (8%)
  between operations  13.5 us (7%)
  matrix products  8.43 us (5%)
    psum x1, waiting for transfers between devices, per_device(): inter = lax.psum(partial_value.astype(jnp.bfloat16), 'rep')  118 us
    all_to_all x1, starting transfers between devices, per_device(): lax.all_to_all(amplitudes, 'tile', split_axis=1, concat_axis=0, tiled=True)  18.8 us
    all_to_all x1, waiting for transfers between devices, per_device(): lax.all_to_all(amplitudes, 'tile', split_axis=1, concat_axis=0, tiled=True)  12.3 us
    dot_general x1, matrix products, per_device(): jnp.einsum('mq,nq->mn', inter, factor_rows, preferred_element_type=jnp.fl...  5.65 us
    unnamed x7, local copies, waits for them, and re-layouts  4.87 us
    reshape x1, local copies, waits for them, and re-layouts, per_device(): factor_rows = factors.reshape(occ_count * second_width, factors.shape[2])  4.53 us
  transfers between devices with their start and end apart: 2, of which 2 were waited for; matrix products, arithmetic and copies ran while one was open for 4% of the time, Pallas kernels for 0%

commit v1 on v0

--- a/solution.py
+++ b/solution.py
@@ -1,10 +1,29 @@
+import functools
+
 import jax
 import jax.numpy as jnp
 from jax import lax
+from jax.experimental import pallas as pl
+from jax.experimental.pallas import tpu as pltpu
 from jax.sharding import PartitionSpec as P
 
-
-def per_device(amplitudes, occ_energy, vir_energy, occ_irrep, vir_irrep, factors):
+X, Z, R = 4, 12, 16
+OCC = 12
+SLAB = 20
+WIDTH = 60
+PAIRS = 3
+GROUPS = 4
+FOLD = SLAB * Z
+NAUX = 2048
+WINDOW = 384
+COLS = GROUPS * 256
+ROWS = 64
+MAIN = 16
+REM = SLAB - MAIN
+F32, BF16, I32 = jnp.float32, jnp.bfloat16, jnp.int32
+
+
+def dense_path(amplitudes, occ_energy, vir_energy, occ_irrep, vir_irrep, factors):
     tile_count = lax.axis_size("tile")
     occ_count = occ_energy.shape[0]
     vir_count = vir_energy.shape[0]
@@ -37,6 +56,330 @@
     return jnp.where(symmetry == 0, relaid.astype(jnp.float32) + cycle / denom, jnp.float32(0.0))
 
 
+def lane_iota(rows):
+    return lax.broadcasted_iota(I32, (rows, 128), 1)
+
+
+def exchange_kernel(
+    amp_hbm, fac_hbm, vir_irrep, vir_energy, occ_irrep, occ_energy,
+    m_out, inter_out, ff_out, row_lab, row_en, col_lab, col_occ, col_vir, flag_out,
+    amp_v, fac_v, pkf, pk, gbuf, part, rsbuf, inter_s, flag_s,
+    load_sem, zsend, zrecv, xsend, xrecv, rsend, rrecv, gsend, grecv,
+):
+    t = lax.axis_index("tile")
+    r = lax.axis_index("rep")
+    x = t // Z
+    z = t % Z
+
+    loads = [pltpu.make_async_copy(amp_hbm.at[j], amp_v.at[j], load_sem.at[j]) for j in range(PAIRS)]
+    loads.append(pltpu.make_async_copy(fac_hbm, fac_v, load_sem.at[PAIRS]))
+    for copy in loads:
+        copy.start()
+
+    barrier = pltpu.get_barrier_semaphore()
+
+    @pl.loop(1, Z)
+    def _(d):
+        pl.semaphore_signal(barrier, inc=1, device_id=(x * Z + (z + d) % Z, r))
+
+    @pl.loop(1, X)
+    def _(d):
+        pl.semaphore_signal(barrier, inc=1, device_id=(((x + d) % X) * Z + z, r))
+
+    @pl.loop(1, R)
+    def _(d):
+        pl.semaphore_signal(barrier, inc=1, device_id=(t, (r + d) % R))
+
+    pkf[...] = jnp.zeros_like(pkf)
+    row = lax.broadcasted_iota(I32, (FOLD, 1), 0)
+    rem_row = row - MAIN * Z
+    target = jnp.where(
+        row < MAIN * Z,
+        SLAB * (row >> 4) + (row & 15),
+        SLAB * (rem_row >> 2) + MAIN + (rem_row & 3),
+    )
+    lane = lax.broadcasted_iota(I32, (1, X * FOLD), 1)
+    folded_lane = lane
+    for n in range(1, X):
+        folded_lane = folded_lane - jnp.where(lane >= n * FOLD, FOLD, 0)
+    pick = jnp.where(target == folded_lane, 1.0, 0.0).astype(BF16)
+    for j in range(PAIRS):
+        loads[j].wait()
+        folded = lax.dot_general(pick, amp_v[j], (((1,), (1,)), ((), ())), preferred_element_type=F32)
+        pkf[:, 64 * j : 64 * j + WIDTH] = folded
+    for n in range(Z):
+        pk[n, :, 0:128] = pkf[MAIN * n : MAIN * (n + 1), 0:128].astype(BF16)
+        base = MAIN * Z + REM * n
+        rem_rows = [pkf[base : base + REM, 128 * (j // 2) : 128 * (j // 2) + 128] for j in range(PAIRS)]
+        rem_rows = [rem_rows[0], pltpu.roll(rem_rows[1], 64, 1), rem_rows[2]]
+        rem = jnp.concatenate(rem_rows + [jnp.zeros((MAIN - PAIRS * REM, 128), F32)], axis=0)
+        rem = jnp.where(lane_iota(MAIN) < 64, rem, 0.0)
+        right = pkf[MAIN * n : MAIN * (n + 1), 128:256] + pltpu.roll(rem, 64, 1)
+        pk[n, :, 128:256] = right.astype(BF16)
+
+    pl.semaphore_wait(barrier, Z - 1 + X - 1 + R - 1)
+
+    def z_send(d):
+        to = (z + d) % Z
+        pltpu.make_async_remote_copy(
+            src_ref=pk.at[to], dst_ref=gbuf.at[t], send_sem=zsend, recv_sem=zrecv.at[z],
+            device_id=(x * Z + to, r),
+        ).start()
+
+    def x_send(slot, d):
+        pltpu.make_async_remote_copy(
+            src_ref=gbuf.at[slot], dst_ref=gbuf.at[slot], send_sem=xsend, recv_sem=xrecv.at[x],
+            device_id=(((x + d) % X) * Z + z, r),
+        ).start()
+
+    gbuf[t] = pk[z]
+
+    @pl.loop(0, Z - 1)
+    def _(n):
+        near = Z // 2 - (n + 1) // 2
+        z_send(jnp.where(n % 2 == 0, near, Z - near))
+
+    for d in range(1, X):
+        x_send(t, d)
+
+    vlane = lax.broadcasted_iota(I32, (24, X * FOLD), 1)
+    vsub = lax.broadcasted_iota(I32, (24, X * FOLD), 0)
+    mine = vlane == SLAB * t + vsub
+    va_lab = jnp.sum(jnp.where(mine, vir_irrep[...].astype(F32), 0.0), axis=1, keepdims=True).astype(I32)
+    va_en = jnp.sum(jnp.where(mine, vir_energy[...], 0.0), axis=1, keepdims=True)
+    for i in range(OCC):
+        n, i3 = i // PAIRS, i % PAIRS
+        lab = jnp.broadcast_to(jnp.bitwise_xor(va_lab, occ_irrep[i]), (24, 128))
+        en = jnp.broadcast_to(occ_energy[i] - va_en, (24, 128))
+        row_lab[n, MAIN * i3 : MAIN * (i3 + 1), :] = lab[:MAIN]
+        row_lab[n, MAIN * PAIRS + REM * i3 : MAIN * PAIRS + REM * (i3 + 1), :] = lab[MAIN:SLAB]
+        row_en[n, MAIN * i3 : MAIN * (i3 + 1), :] = en[:MAIN]
+        row_en[n, MAIN * PAIRS + REM * i3 : MAIN * PAIRS + REM * (i3 + 1), :] = en[MAIN:SLAB]
+    for n in range(X):
+        row_lab[n, ROWS - REM : ROWS, :] = jnp.full((REM, 128), -1, I32)
+        row_en[n, ROWS - REM : ROWS, :] = jnp.zeros((REM, 128), F32)
+
+    pad = jnp.zeros((8, 1024 - X * FOLD), F32)
+    shift = (1024 - WIDTH * r) % 1024
+    lane8 = lane_iota(8)
+    half = lane8 & 63
+
+    def columns(values):
+        whole = jnp.concatenate([jnp.broadcast_to(values, (8, X * FOLD)), pad], axis=1)
+        mine = jnp.where(lane8 < WIDTH, pltpu.roll(whole, shift, 1)[:, :128], 0.0)
+        return mine + pltpu.roll(mine, 64, 1)
+
+    vb_lab = columns(vir_irrep[...].astype(F32)).astype(I32)
+    vb_en = columns(vir_energy[...])
+    for g in range(GROUPS):
+        for h in range(2):
+            first = PAIRS * g + 2 * h
+            second = min(first + 1, PAIRS * g + 2)
+            cols = slice(256 * g + 128 * h, 256 * g + 128 * h + 128)
+            lab = jnp.bitwise_xor(vb_lab, jnp.where(lane8 < 64, occ_irrep[first], occ_irrep[second]))
+            valid = (half < WIDTH) & ((lane8 < 64) | (h == 0))
+            col_lab[:, cols] = jnp.where(valid, lab, -2)
+            col_occ[:, cols] = jnp.where(lane8 < 64, occ_energy[first], occ_energy[second])
+            col_vir[:, cols] = vb_en
+
+    @pl.loop(0, Z - 1)
+    def _(n):
+        near = n // 2 + 1
+        slot = x * Z + (z + jnp.where(n % 2 == 0, near, Z - near)) % Z
+        pltpu.make_async_copy(gbuf.at[slot], gbuf.at[slot], zrecv.at[slot - x * Z]).wait()
+        for d in range(1, X):
+            x_send(slot, d)
+
+    loads[PAIRS].wait()
+    zero4 = jnp.zeros((64 - WIDTH, WINDOW), F32)
+    for g in range(GROUPS):
+        ff_out[256 * g + 192 : 256 * (g + 1), :] = jnp.zeros((64, WINDOW), BF16)
+    for k in range(OCC):
+        base = 256 * (k // PAIRS) + 64 * (k % PAIRS)
+        total = fac_v[k, :, 0:WINDOW].astype(F32)
+        for n in range(1, NAUX // WINDOW):
+            total = total + fac_v[k, :, WINDOW * n : WINDOW * (n + 1)].astype(F32)
+        last = NAUX // WINDOW * WINDOW
+        tail = fac_v[k, :, last:NAUX].astype(F32)
+        total = total + jnp.concatenate([tail, jnp.zeros((WIDTH, WINDOW - NAUX + last), F32)], axis=1)
+        ff_out[base : base + 64, :] = jnp.concatenate([total, zero4], axis=0).astype(BF16)
+
+    vlane8 = lax.broadcasted_iota(I32, (8, X * FOLD), 1)
+    vsub8 = lax.broadcasted_iota(I32, (8, X * FOLD), 0)
+    first_lab = jnp.sum(
+        jnp.where(vlane8 == WIDTH * r + vsub8, vir_irrep[...].astype(F32), 0.0), axis=1, keepdims=True
+    ).astype(I32)
+    seen = jnp.zeros((8, NAUX), I32)
+    for k in range(OCC):
+        bit = jnp.left_shift(jnp.int32(1), jnp.bitwise_xor(first_lab, occ_irrep[k]))
+        seen = jnp.bitwise_or(seen, jnp.where(fac_v[k, 0:16, :].astype(F32)[0:8] != 0.0, bit, 0))
+    for n in (4, 2, 1):
+        seen = jnp.bitwise_or(seen, pltpu.roll(seen, n, 0))
+    seen = seen[0:1]
+    bad = jnp.zeros((1, 1), F32)
+    covered = jnp.zeros((1, 1), F32)
+    for h in range(8):
+        aux_size = jnp.sum(jnp.where(seen == (1 << h), 1.0, 0.0), axis=1, keepdims=True)
+        vir_size = jnp.sum(jnp.where(vir_irrep[...] == h, 1.0, 0.0), axis=1, keepdims=True)
+        covered = covered + aux_size
+        bad = bad + jnp.where(aux_size > WINDOW, 1.0, 0.0) + jnp.where(vir_size > FOLD, 1.0, 0.0)
+    bad = bad + jnp.where(covered != NAUX, 1.0, 0.0)
+    flag_s[...] = jnp.broadcast_to(jnp.where(bad > 0.0, 1.0, 0.0), (8, 128))
+
+    @pl.loop(0, X)
+    def _(d):
+        xs = (x + d) % X
+
+        @pl.when(d > 0)
+        def _():
+            block = gbuf.at[pl.ds(xs * Z, Z)]
+            pltpu.make_async_copy(block, block, xrecv.at[xs]).wait()
+
+        for g in range(GROUPS):
+            blocks = [gbuf[xs * Z + GROUPS * i3 + g].astype(F32) for i3 in range(PAIRS)]
+            cols = slice(256 * g, 256 * (g + 1))
+            clab = col_lab[0:1, cols]
+            for i3 in range(PAIRS):
+                rows = slice(MAIN * i3, MAIN * (i3 + 1))
+                rlab = jnp.concatenate([row_lab[xs, rows, :]] * 2, axis=1)
+                m_out[xs, rows, cols] = jnp.where(rlab == clab, blocks[i3], 0.0).astype(BF16)
+            pieces = []
+            for j in range(PAIRS):
+                rem = [b[REM * j : REM * (j + 1), 128:256] for b in blocks]
+                pieces.append(jnp.concatenate(rem + [jnp.zeros((REM, 128), F32)], axis=0))
+            low = lane_iota(MAIN) < 64
+            left = jnp.where(low, pltpu.roll(pieces[0], 64, 1), pieces[1])
+            right = jnp.where(low, pltpu.roll(pieces[2], 64, 1), 0.0)
+            rows = slice(MAIN * PAIRS, ROWS)
+            rlab = jnp.concatenate([row_lab[xs, rows, :]] * 2, axis=1)
+            whole = jnp.concatenate([left, right], axis=1)
+            m_out[xs, rows, cols] = jnp.where(rlab == clab, whole, 0.0).astype(BF16)
+        res = jnp.dot(m_out[xs], ff_out[...], preferred_element_type=F32)
+        sub = lax.broadcasted_iota(I32, (ROWS, WINDOW), 0)
+        res = jnp.where(sub < ROWS - REM, res, flag_s[0:1, 0:1]).astype(BF16)
+        for c in range(4):
+            e = 4 * xs + c
+            part[e] = res[MAIN * c : MAIN * (c + 1)]
+
+            @pl.when(e != r)
+            def _():
+                pltpu.make_async_remote_copy(
+                    src_ref=part.at[e], dst_ref=rsbuf.at[r], send_sem=rsend, recv_sem=rrecv,
+                    device_id=(t, e),
+                ).start()
+
+    rsbuf[r] = part[r]
+    rest = rsbuf.at[pl.ds(0, R - 1)]
+    pltpu.make_async_copy(rest, rest, rrecv).wait()
+    total = rsbuf[0].astype(F32)
+    for n in range(1, R):
+        total = total + rsbuf[n].astype(F32)
+    inter_s[r] = total.astype(BF16)
+
+    @pl.loop(1, R)
+    def _(d):
+        pltpu.make_async_remote_copy(
+            src_ref=inter_s.at[r], dst_ref=inter_s.at[r], send_sem=gsend, recv_sem=grecv,
+            device_id=(t, (r + d) % R),
+        ).start()
+
+    rest = inter_s.at[pl.ds(0, R - 1)]
+    pltpu.make_async_copy(rest, rest, grecv).wait()
+    inter_out[...] = inter_s[...]
+    flag_out[...] = inter_s[3].astype(F32)[8:16, 0:128]
+
+    sent = pk.at[pl.ds(0, Z - 1)]
+    pltpu.make_async_copy(sent, sent, zsend).wait()
+    sent = gbuf.at[pl.ds(0, Z * (X - 1))]
+    pltpu.make_async_copy(sent, sent, xsend).wait()
+    sent = part.at[pl.ds(0, R - 1)]
+    pltpu.make_async_copy(sent, sent, rsend).wait()
+    sent = inter_s.at[pl.ds(0, R - 1)]
+    pltpu.make_async_copy(sent, sent, gsend).wait()
+
+
+def exchange(amplitudes, occ_energy, vir_energy, occ_irrep, vir_irrep, factors):
+    vmem = pl.BlockSpec(memory_space=pltpu.VMEM)
+    smem = pl.BlockSpec(memory_space=pltpu.SMEM)
+    hbm = pl.BlockSpec(memory_space=pl.ANY)
+    shapes = [
+        ((X, ROWS, COLS), BF16),
+        ((R, MAIN, WINDOW), BF16),
+        ((COLS, WINDOW), BF16),
+        ((X, ROWS, 128), I32),
+        ((X, ROWS, 128), F32),
+        ((8, COLS), I32),
+        ((8, COLS), F32),
+        ((8, COLS), F32),
+        ((8, 128), F32),
+    ]
+    dma = pltpu.SemaphoreType.DMA
+    return pl.pallas_call(
+        exchange_kernel,
+        out_shape=[jax.ShapeDtypeStruct(*s) for s in shapes],
+        in_specs=[hbm, hbm, vmem, vmem, smem, smem],
+        out_specs=[vmem] * len(shapes),
+        scratch_shapes=[
+            pltpu.VMEM((PAIRS, WIDTH, X * FOLD), BF16),
+            pltpu.VMEM((OCC, WIDTH, NAUX), BF16),
+            pltpu.VMEM((FOLD, 256), F32),
+            pltpu.VMEM((Z, MAIN, 256), BF16),
+            pltpu.VMEM((X * Z, MAIN, 256), BF16),
+            pltpu.VMEM((R, MAIN, WINDOW), BF16),
+            pltpu.VMEM((R, MAIN, WINDOW), BF16),
+            pltpu.VMEM((R, MAIN, WINDOW), BF16),
+            pltpu.VMEM((8, 128), F32),
+            dma((PAIRS + 1,)), dma, dma((Z,)), dma, dma((X,)), dma, dma, dma, dma,
+        ],
+        compiler_params=pltpu.CompilerParams(
+            collective_id=0, has_side_effects=True, vmem_limit_bytes=32 * 1024 * 1024
+        ),
+        name="exchange",
+    )(
+        amplitudes.transpose(0, 2, 1), factors, vir_irrep.reshape(1, -1), vir_energy.reshape(1, -1),
+        occ_irrep, occ_energy,
+    )
+
+
+def finish_kernel(m_ref, inter_ref, ff_ref, row_lab, row_en, col_lab, col_occ, col_vir, out, res):
+    for n in range(X):
+        inter = jnp.concatenate([inter_ref[4 * n + c] for c in range(4)], axis=0)
+        cycle = lax.dot_general(inter, ff_ref[...], (((1,), (1,)), ((), ())), preferred_element_type=F32)
+        for g in range(GROUPS):
+            cols = slice(256 * g, 256 * (g + 1))
+            rlab = jnp.concatenate([row_lab[n]] * 2, axis=1)
+            ren = jnp.concatenate([row_en[n]] * 2, axis=1)
+            denom = ren + col_occ[0:1, cols] - col_vir[0:1, cols]
+            value = m_ref[n, :, cols].astype(F32) + cycle[:, cols] / denom
+            res[:, cols] = jnp.where(rlab == col_lab[0:1, cols], value, 0.0)
+        for i3 in range(PAIRS):
+            i = PAIRS * n + i3
+            for j in range(OCC):
+                base = 256 * (j // PAIRS) + 64 * (j % PAIRS)
+                out[i, j, 0:MAIN, :] = res[MAIN * i3 : MAIN * (i3 + 1), base : base + WIDTH]
+                rem = MAIN * PAIRS + REM * i3
+                out[i, j, MAIN:SLAB, :] = res[rem : rem + REM, base : base + WIDTH]
+
+
+def finish(*operands):
+    vmem = pl.BlockSpec(memory_space=pltpu.VMEM)
+    out = pl.pallas_call(
+        finish_kernel,
+        out_shape=jax.ShapeDtypeStruct((OCC, OCC, SLAB, WIDTH), F32),
+        in_specs=[vmem] * 8,
+        out_specs=vmem,
+        scratch_shapes=[pltpu.VMEM((ROWS, COLS), F32)],
+        compiler_params=pltpu.CompilerParams(vmem_limit_bytes=32 * 1024 * 1024),
+        name="finish",
+    )(*operands)
+    return out.transpose(0, 2, 1, 3)
+
+
+def per_device(*arguments):
+    *operands, flag = exchange(*arguments)
+    return lax.cond(flag[7, 0] == 0.0, lambda: finish(*operands), lambda: dense_path(*arguments))
+
+
 def solution(mesh):
     return jax.shard_map(
         per_device,

time: 186 us -> 69.2 us (0.37)
  waiting for transfers between devices: 130 us -> 0 us
  Pallas kernels: 0 us -> 53.2 us
  starting transfers between devices: 18.9 us -> 0 us
  local copies, waits for them, and re-layouts: 14.8 us -> 1.73 us
  matrix products: 8.43 us -> 0 us
    psum x1 -> x0, waiting for transfers between devices: 118 us -> none  [per_device(): inter = lax.psum(partial_value.astype(jnp.bfloat16), 'rep')]
    pallas_call x0 -> x2, Pallas kernels: none -> 53.2 us  [the longest x1 50.4 us: exchange(): pl.pallas_call(exchange_kernel, out_shape=[jax.ShapeDtypeStruct(*s) for s...]
    all_to_all x1 -> x0, starting transfers between devices: 18.8 us -> none  [per_device(): lax.all_to_all(amplitudes, 'tile', split_axis=1, concat_axis=0, tiled=True)]
    all_to_all x1 -> x0, waiting for transfers between devices: 12.3 us -> none  [per_device(): lax.all_to_all(amplitudes, 'tile', split_axis=1, concat_axis=0, tiled=True)]
    dot_general x2 -> x0, matrix products: 8.43 us -> none  [the longest x1 5.65 us: per_device(): jnp.einsum('mq,nq->mn', inter, factor_rows, preferred_element_type=jnp.fl...]
    reshape x2 -> x0, local copies, waits for them, and re-layouts: 5.44 us -> none  [the longest x1 4.53 us: per_device(): factor_rows = factors.reshape(occ_count * second_width, factors.shape[2])]
    unnamed x7 -> x10, local copies, waits for them, and re-layouts: 4.87 us -> 1.22 us
    dynamic_slice x4 -> x0, local copies, waits for them, and re-layouts: 3.04 us -> none  [the longest x1 0.76 us: per_device(): vir_second = lax.dynamic_slice_in_dim(vir_energy, rep_start, second_width)]
  transfers between devices with their start and end apart: 2 -> 0, of which waited for: 2 -> 0; matrix products, arithmetic and copies ran while one was open for 4% -> 0% of each run, Pallas kernels for 0% -> 0%
where the time goes in v1:
time: 69.2 us; the launch traced here: 69 us
  Pallas kernels  53.2 us (77%)
  between operations  14.1 us (20%)
  local copies, waits for them, and re-layouts  1.73 us (2%)
    pallas_call x1, Pallas kernels, exchange(): pl.pallas_call(exchange_kernel, out_shape=[jax.ShapeDtypeStruct(*s) for s...  50.4 us
    pallas_call x1, Pallas kernels, finish(): pl.pallas_call(finish_kernel, out_shape=jax.ShapeDtypeStruct((OCC, OCC, S...  2.74 us

profile of v1, /device:TPU:1, one launch (start us, length us, event | category | flops | bytes accessed | tf_op | source)
XLA Modules:
  0.0 69.0 jit_solution(573486664894849430)
XLA Ops:
  6.5 0.0 copy-start
  6.5 0.0 copy-start.2
  6.5 0.0 copy-start.3
  6.5 0.0 copy-start.4
  6.5 50.4 %exchange.1 = (bf16[4,64,1024]{2,1,0:T(8,128)(2,1)}, bf16[16,16,384]{2,1,0:T(8,128)(2,1)}, bf16[1024,384]{1,0:T(8,128)(2,1)}, s32[4,64,128]{2,1,0:T(8,128)}, f32...) custom-call(bf16[3,60,960]{2,1,0:T(8,128)(2,1)} %bitcast.30, ...), custom_call_target="tpu_custom_call" | custom-call | tf_op jit(solution)/shard_map/exchange/pallas_call | solution.py:317
  57.0 0.5 slice.3
  58.2 0.0 copy-done
  58.2 0.0 copy-done.2
  58.2 0.0 copy-done.3
  58.2 0.0 copy-done.4
  58.2 2.8 %conditional.1 = (f32[12,20,12,60]{3,1,2,0:T(8,128)S(1)}) conditional(s32[]{:T(128)} %bitcast.14, (s32[12]{0:T(128)S(1)}, s32[960]{0:T(1024)}, bf16[3,960,60]{1,2,0:T(8,128)(2,1)S(1)}, bf16[12,60,2048]{2,1,0:T(8,128)(2,1)S(1)}, f32[12]{0:T(128)S(1)}, /*index=5*/f32[960]{0:T(1024)}) %tuple.25, (bf16[4,64,1024]{2,1,0:T(8,128)(2,1)}, ...), branch_computations={%region_0.2_spmd, %region_2.3_spmd} | conditional | flops 1417774336 | bytes 30049992 | solution.py:380
  58.2 2.7 %finish.1 = f32[12,12,20,60]{3,2,1,0:T(8,128)S(1)} custom-call(bf16[4,64,1024]{2,1,0:T(8,128)(2,1)} %get-tuple-element.42.m_ref, bf16[16,16,384]{2,1,0:T(8,128)(2,1)} %get-tuple-element.43.inter_ref, bf16[1024,384]{1,0:T(8,128)(2,1)} %get-tuple-element.44.ff_ref, s32[4,64,128]{2,1,0:T(8,128)} %get-tuple-element.45.row_lab, ...), custom_call_target="tpu_custom_call" | custom-call | tf_op jit(solution)/shard_map/cond/branch_1_fun/finish/pallas_call | solution.py:366
  61.0 0.0 copy-start.5
  61.0 1.2 %copy-done.5 = f32[12,20,12,60]{3,1,2,0:T(8,128)} copy-done((f32[12,20,12,60]{3,1,2,0:T(8,128)}, f32[12,20,12,60]{3,1,2,0:T(8,128)S(1)}, u32[]{:S(2)}) %copy-start.5) | copy-done | bytes 691224
Async XLA Ops:
  6.5 51.6 %copy-start = (bf16[12,60,2048]{2,1,0:T(8,128)(2,1)S(1)}, bf16[12,60,2048]{2,1,0:T(8,128)(2,1)}, u32[]{:S(2)}) copy-start(bf16[12,60,2048]{2,1,0:T(8,128)(2,1)} %fac_hbm.1) | copy-start | bytes 8847364
  6.5 51.6 %copy-start.2 = (bf16[3,960,60]{1,2,0:T(8,128)(2,1)S(1)}, bf16[3,960,60]{1,2,0:T(8,128)(2,1)}, u32[]{:S(2)}) copy-start(bf16[3,960,60]{1,2,0:T(8,128)(2,1)} %param.8) | copy-start | bytes 1036804
  6.5 51.6 %copy-start.3 = (f32[12]{0:T(128)S(1)}, f32[12]{0:T(128)}, u32[]{:S(2)}) copy-start(f32[12]{0:T(128)} %occ_energy.1) | copy-start | bytes 148
  6.5 51.7 %copy-start.4 = (s32[12]{0:T(128)S(1)}, s32[12]{0:T(128)}, u32[]{:S(2)}) copy-start(s32[12]{0:T(128)} %occ_irrep.1) | copy-start | bytes 148
  61.0 1.2 %copy-start.5 = (f32[12,20,12,60]{3,1,2,0:T(8,128)}, f32[12,20,12,60]{3,1,2,0:T(8,128)S(1)}, u32[]{:S(2)}) copy-start(f32[12,20,12,60]{3,1,2,0:T(8,128)S(1)} %get-tuple-element.96) | copy-start | bytes 2073604

commit v2 on v1

--- a/solution.py
+++ b/solution.py
@@ -60,16 +60,45 @@
     return lax.broadcasted_iota(I32, (rows, 128), 1)
 
 
+def assemble(dst, blocks, rows, bcol):
+    low = lane_iota(MAIN) < 64
+    for g in range(GROUPS):
+        cols = slice(256 * g, 256 * (g + 1))
+        kept = [
+            jnp.where(rows[i3] == bcol[g], blocks[GROUPS * i3 + g].astype(F32), 0.0) for i3 in range(PAIRS)
+        ]
+        for i3 in range(PAIRS):
+            dst[MAIN * i3 : MAIN * (i3 + 1), cols] = kept[i3].astype(BF16)
+        pieces = []
+        for j in range(PAIRS):
+            rem = [v[REM * j : REM * (j + 1), 128:256] for v in kept]
+            pieces.append(jnp.concatenate(rem + [jnp.zeros((REM, 128), F32)], axis=0))
+        left = jnp.where(low, pltpu.roll(pieces[0], 64, 1), pieces[1])
+        right = jnp.where(low, pltpu.roll(pieces[2], 64, 1), 0.0)
+        dst[MAIN * PAIRS : ROWS, cols] = jnp.concatenate([left, right], axis=1).astype(BF16)
+
+
+def block_rows(lab, occ):
+    main = jnp.broadcast_to(jnp.bitwise_xor(lab[:MAIN], occ), (MAIN, 128))
+    rem = jnp.bitwise_xor(lab[MAIN:SLAB], occ)
+    rem = jnp.concatenate([rem] * PAIRS + [jnp.full((MAIN - PAIRS * REM, 1), -1, I32)], axis=0)
+    right = jnp.where(lane_iota(MAIN) < 64, main, jnp.broadcast_to(rem, (MAIN, 128)))
+    return jnp.concatenate([main, right], axis=1)
+
+
 def exchange_kernel(
     amp_hbm, fac_hbm, vir_irrep, vir_energy, occ_irrep, occ_energy,
     m_out, inter_out, ff_out, row_lab, row_en, col_lab, col_occ, col_vir, flag_out,
-    amp_v, fac_v, pkf, pk, gbuf, part, rsbuf, inter_s, flag_s,
-    load_sem, zsend, zrecv, xsend, xrecv, rsend, rrecv, gsend, grecv,
+    amp_v, fac_v, pkf, pk, gbuf, bcol, brow, ms, part, cbuf, send, rsbuf, inter_s, flag_s,
+    load_sem, zsend, zrecv, xsend, xrecv, csend, crecv, rsend, rrecv, gsend, grecv, fsend, frecv,
 ):
     t = lax.axis_index("tile")
     r = lax.axis_index("rep")
     x = t // Z
     z = t % Z
+    y = r // 2
+    core = r % 2
+    sibling = (t, 2 * y + 1 - core)
 
     loads = [pltpu.make_async_copy(amp_hbm.at[j], amp_v.at[j], load_sem.at[j]) for j in range(PAIRS)]
     loads.append(pltpu.make_async_copy(fac_hbm, fac_v, load_sem.at[PAIRS]))
@@ -78,17 +107,30 @@
 
     barrier = pltpu.get_barrier_semaphore()
 
-    @pl.loop(1, Z)
+    def z_peer(n):
+        near = Z // 2 - (n + 1) // 2
+        return (z + jnp.where(n % 2 == 0, near, Z - near)) % Z
+
+    @pl.loop(0, Z - 1)
+    def _(n):
+        pl.semaphore_signal(barrier, inc=1, device_id=(x * Z + z_peer(n), r))
+
+    def reducer(d, h):
+        return 2 * (2 * ((x + d) % X) + h) + core
+
+    origin = (y // 2 - x + X) % X
+    mine_h = y % 2
+    chunk = 4 * origin + 2 * core + mine_h
+
+    @pl.loop(0, X)
     def _(d):
-        pl.semaphore_signal(barrier, inc=1, device_id=(x * Z + (z + d) % Z, r))
-
-    @pl.loop(1, X)
-    def _(d):
-        pl.semaphore_signal(barrier, inc=1, device_id=(((x + d) % X) * Z + z, r))
-
-    @pl.loop(1, R)
-    def _(d):
-        pl.semaphore_signal(barrier, inc=1, device_id=(t, (r + d) % R))
+        @pl.loop(0, R // 2)
+        def _(n):
+            @pl.when((d != x) | (n != y))
+            def _():
+                pl.semaphore_signal(barrier, inc=1, device_id=(d * Z + z, 2 * n + core))
+
+    pl.semaphore_signal(barrier, inc=1, device_id=sibling)
 
     pkf[...] = jnp.zeros_like(pkf)
     row = lax.broadcasted_iota(I32, (FOLD, 1), 0)
@@ -117,38 +159,34 @@
         right = pkf[MAIN * n : MAIN * (n + 1), 128:256] + pltpu.roll(rem, 64, 1)
         pk[n, :, 128:256] = right.astype(BF16)
 
-    pl.semaphore_wait(barrier, Z - 1 + X - 1 + R - 1)
-
-    def z_send(d):
-        to = (z + d) % Z
+    pl.semaphore_wait(barrier, Z - 1 + X * (R // 2) - 1 + 1)
+
+    @pl.loop(0, Z - 1)
+    def _(n):
+        to = z_peer(n)
         pltpu.make_async_remote_copy(
-            src_ref=pk.at[to], dst_ref=gbuf.at[t], send_sem=zsend, recv_sem=zrecv.at[z],
+            src_ref=pk.at[to], dst_ref=gbuf.at[x, z], send_sem=zsend, recv_sem=zrecv,
             device_id=(x * Z + to, r),
         ).start()
 
-    def x_send(slot, d):
-        pltpu.make_async_remote_copy(
-            src_ref=gbuf.at[slot], dst_ref=gbuf.at[slot], send_sem=xsend, recv_sem=xrecv.at[x],
-            device_id=(((x + d) % X) * Z + z, r),
-        ).start()
-
-    gbuf[t] = pk[z]
-
-    @pl.loop(0, Z - 1)
-    def _(n):
-        near = Z // 2 - (n + 1) // 2
-        z_send(jnp.where(n % 2 == 0, near, Z - near))
-
-    for d in range(1, X):
-        x_send(t, d)
+    gbuf[x, z] = pk[z]
 
     vlane = lax.broadcasted_iota(I32, (24, X * FOLD), 1)
     vsub = lax.broadcasted_iota(I32, (24, X * FOLD), 0)
-    mine = vlane == SLAB * t + vsub
-    va_lab = jnp.sum(jnp.where(mine, vir_irrep[...].astype(F32), 0.0), axis=1, keepdims=True).astype(I32)
-    va_en = jnp.sum(jnp.where(mine, vir_energy[...], 0.0), axis=1, keepdims=True)
+    virs = vir_irrep[...].astype(F32)
+
+    def slab_values(tile, values):
+        return jnp.sum(jnp.where(vlane == SLAB * tile + vsub, values, 0.0), axis=1, keepdims=True)
+
+    for n in range(X):
+        lab = slab_values(n * Z + z, virs).astype(I32)
+        for i3 in range(PAIRS):
+            brow[n, i3] = block_rows(lab, occ_irrep[PAIRS * x + i3])
+    va_lab = slab_values(t, virs).astype(I32)
+    va_en = slab_values(t, vir_energy[...])
     for i in range(OCC):
         n, i3 = i // PAIRS, i % PAIRS
+        brow[X + n, i3] = block_rows(va_lab, occ_irrep[i])
         lab = jnp.broadcast_to(jnp.bitwise_xor(va_lab, occ_irrep[i]), (24, 128))
         en = jnp.broadcast_to(occ_energy[i] - va_en, (24, 128))
         row_lab[n, MAIN * i3 : MAIN * (i3 + 1), :] = lab[:MAIN]
@@ -169,26 +207,27 @@
         mine = jnp.where(lane8 < WIDTH, pltpu.roll(whole, shift, 1)[:, :128], 0.0)
         return mine + pltpu.roll(mine, 64, 1)
 
-    vb_lab = columns(vir_irrep[...].astype(F32)).astype(I32)
+    vb_lab = columns(virs).astype(I32)
     vb_en = columns(vir_energy[...])
+    sub16 = lax.broadcasted_iota(I32, (MAIN, 128), 0)
+    vb_lab16 = jnp.concatenate([vb_lab, vb_lab], axis=0)
     for g in range(GROUPS):
         for h in range(2):
             first = PAIRS * g + 2 * h
             second = min(first + 1, PAIRS * g + 2)
             cols = slice(256 * g + 128 * h, 256 * g + 128 * h + 128)
             lab = jnp.bitwise_xor(vb_lab, jnp.where(lane8 < 64, occ_irrep[first], occ_irrep[second]))
-            valid = (half < WIDTH) & ((lane8 < 64) | (h == 0))
-            col_lab[:, cols] = jnp.where(valid, lab, -2)
+            lab = jnp.where(half < WIDTH, lab, -2)
+            col_lab[:, cols] = jnp.where((lane8 < 64) | (h == 0), lab, -2)
             col_occ[:, cols] = jnp.where(lane8 < 64, occ_energy[first], occ_energy[second])
             col_vir[:, cols] = vb_en
-
-    @pl.loop(0, Z - 1)
-    def _(n):
-        near = n // 2 + 1
-        slot = x * Z + (z + jnp.where(n % 2 == 0, near, Z - near)) % Z
-        pltpu.make_async_copy(gbuf.at[slot], gbuf.at[slot], zrecv.at[slot - x * Z]).wait()
-        for d in range(1, X):
-            x_send(slot, d)
+            lab = jnp.concatenate([lab, lab], axis=0)
+            if h == 1:
+                occ = [occ_irrep[PAIRS * g + j] for j in range(PAIRS)]
+                occ = jnp.where(sub16 < REM, occ[0], jnp.where(sub16 < 2 * REM, occ[1], occ[2]))
+                rem = jnp.where((lane_iota(MAIN) & 63) < WIDTH, jnp.bitwise_xor(vb_lab16, occ), -2)
+                lab = jnp.where(lane_iota(MAIN) < 64, lab, rem)
+            bcol[g, :, 128 * h : 128 * h + 128] = lab
 
     loads[PAIRS].wait()
     zero4 = jnp.zeros((64 - WIDTH, WINDOW), F32)
@@ -207,7 +246,7 @@
     vlane8 = lax.broadcasted_iota(I32, (8, X * FOLD), 1)
     vsub8 = lax.broadcasted_iota(I32, (8, X * FOLD), 0)
     first_lab = jnp.sum(
-        jnp.where(vlane8 == WIDTH * r + vsub8, vir_irrep[...].astype(F32), 0.0), axis=1, keepdims=True
+        jnp.where(vlane8 == WIDTH * r + vsub8, virs, 0.0), axis=1, keepdims=True
     ).astype(I32)
     seen = jnp.zeros((8, NAUX), I32)
     for k in range(OCC):
@@ -226,76 +265,112 @@
     bad = bad + jnp.where(covered != NAUX, 1.0, 0.0)
     flag_s[...] = jnp.broadcast_to(jnp.where(bad > 0.0, 1.0, 0.0), (8, 128))
 
-    @pl.loop(0, X)
-    def _(d):
-        xs = (x + d) % X
-
-        @pl.when(d > 0)
-        def _():
-            block = gbuf.at[pl.ds(xs * Z, Z)]
-            pltpu.make_async_copy(block, block, xrecv.at[xs]).wait()
-
-        for g in range(GROUPS):
-            blocks = [gbuf[xs * Z + GROUPS * i3 + g].astype(F32) for i3 in range(PAIRS)]
-            cols = slice(256 * g, 256 * (g + 1))
-            clab = col_lab[0:1, cols]
-            for i3 in range(PAIRS):
-                rows = slice(MAIN * i3, MAIN * (i3 + 1))
-                rlab = jnp.concatenate([row_lab[xs, rows, :]] * 2, axis=1)
-                m_out[xs, rows, cols] = jnp.where(rlab == clab, blocks[i3], 0.0).astype(BF16)
-            pieces = []
-            for j in range(PAIRS):
-                rem = [b[REM * j : REM * (j + 1), 128:256] for b in blocks]
-                pieces.append(jnp.concatenate(rem + [jnp.zeros((REM, 128), F32)], axis=0))
-            low = lane_iota(MAIN) < 64
-            left = jnp.where(low, pltpu.roll(pieces[0], 64, 1), pieces[1])
-            right = jnp.where(low, pltpu.roll(pieces[2], 64, 1), 0.0)
-            rows = slice(MAIN * PAIRS, ROWS)
-            rlab = jnp.concatenate([row_lab[xs, rows, :]] * 2, axis=1)
-            whole = jnp.concatenate([left, right], axis=1)
-            m_out[xs, rows, cols] = jnp.where(rlab == clab, whole, 0.0).astype(BF16)
-        res = jnp.dot(m_out[xs], ff_out[...], preferred_element_type=F32)
-        sub = lax.broadcasted_iota(I32, (ROWS, WINDOW), 0)
+    peers = gbuf.at[x, pl.ds(0, Z - 1)]
+    pltpu.make_async_copy(peers, peers, zrecv).wait()
+    blocks = [gbuf[x, n] for n in range(Z)]
+    cols = [bcol[g] for g in range(GROUPS)]
+    for n in range(X):
+        assemble(ms.at[pl.ds(ROWS * n, ROWS)], blocks, [brow[n, i3] for i3 in range(PAIRS)], cols)
+    sub = lax.broadcasted_iota(I32, (ROWS, WINDOW), 0)
+    for n in range(X):
+        rows = slice(ROWS * n, ROWS * (n + 1))
+        res = jnp.dot(ms[rows], ff_out[...], preferred_element_type=F32)
         res = jnp.where(sub < ROWS - REM, res, flag_s[0:1, 0:1]).astype(BF16)
-        for c in range(4):
-            e = 4 * xs + c
-            part[e] = res[MAIN * c : MAIN * (c + 1)]
-
-            @pl.when(e != r)
+        part[0, n] = res[: ROWS // 2]
+        part[1, n] = res[ROWS // 2 :]
+
+    swap = pltpu.make_async_remote_copy(
+        src_ref=part.at[1 - core], dst_ref=cbuf, send_sem=csend, recv_sem=crecv, device_id=sibling
+    )
+    swap.start()
+    swap.wait_recv()
+    for n in range(X):
+        total = (part[core, n].astype(F32) + cbuf[n].astype(F32)).astype(BF16)
+        send[n, 0] = total[:MAIN]
+        send[n, 1] = total[MAIN:]
+
+    for n in range(X):
+        for h in range(2):
+            to = reducer(n, h)
+
+            @pl.when((n != x) | (to != r))
             def _():
                 pltpu.make_async_remote_copy(
-                    src_ref=part.at[e], dst_ref=rsbuf.at[r], send_sem=rsend, recv_sem=rrecv,
-                    device_id=(t, e),
+                    src_ref=send.at[n, h], dst_ref=rsbuf.at[y], send_sem=rsend, recv_sem=rrecv,
+                    device_id=(n * Z + z, to),
                 ).start()
 
-    rsbuf[r] = part[r]
-    rest = rsbuf.at[pl.ds(0, R - 1)]
-    pltpu.make_async_copy(rest, rest, rrecv).wait()
+    for d in (1, 3, 2):
+        pltpu.make_async_remote_copy(
+            src_ref=gbuf.at[x], dst_ref=gbuf.at[x], send_sem=xsend, recv_sem=xrecv.at[x],
+            device_id=(((x + d) % X) * Z + z, r),
+        ).start()
+    assemble(m_out.at[x], blocks, [brow[X + x, i3] for i3 in range(PAIRS)], cols)
+
+    own = origin == x
+
+    @pl.when(own)
+    def _():
+        rsbuf[y] = send[x, mine_h]
+        rest = rsbuf.at[pl.ds(0, R // 2 - 1)]
+        pltpu.make_async_copy(rest, rest, rrecv).wait()
+        pltpu.make_async_copy(rest, rest, rsend).wait()
+
+    @pl.when(jnp.logical_not(own))
+    def _():
+        pltpu.make_async_copy(rsbuf, rsbuf, rrecv).wait()
+        pltpu.make_async_copy(rsbuf, rsbuf, rsend).wait()
+
     total = rsbuf[0].astype(F32)
-    for n in range(1, R):
+    for n in range(1, R // 2):
         total = total + rsbuf[n].astype(F32)
-    inter_s[r] = total.astype(BF16)
-
-    @pl.loop(1, R)
-    def _(d):
+    inter_s[chunk] = total.astype(BF16)
+
+    @pl.loop(0, R // 2 - 1)
+    def _(n):
+        near = (R // 4) - (n + 1) // 2
+        to = (y + jnp.where(n % 2 == 0, near, R // 2 - near)) % (R // 2)
         pltpu.make_async_remote_copy(
-            src_ref=inter_s.at[r], dst_ref=inter_s.at[r], send_sem=gsend, recv_sem=grecv,
-            device_id=(t, (r + d) % R),
+            src_ref=inter_s.at[chunk], dst_ref=inter_s.at[chunk], send_sem=gsend, recv_sem=grecv.at[y],
+            device_id=(t, 2 * to + core),
         ).start()
 
-    rest = inter_s.at[pl.ds(0, R - 1)]
-    pltpu.make_async_copy(rest, rest, grecv).wait()
+    def hand_on(slot):
+        pltpu.make_async_remote_copy(
+            src_ref=inter_s.at[slot], dst_ref=inter_s.at[slot], send_sem=fsend, recv_sem=frecv,
+            device_id=sibling,
+        ).start()
+
+    hand_on(chunk)
+
+    for d in (1, 3, 2):
+        xs = (x + d) % X
+        pltpu.make_async_copy(gbuf.at[xs], gbuf.at[xs], xrecv.at[xs]).wait()
+        assemble(
+            m_out.at[xs], [gbuf[xs, n] for n in range(Z)], [brow[X + xs, i3] for i3 in range(PAIRS)], cols
+        )
+
+    @pl.loop(0, R // 2 - 1)
+    def _(n):
+        near = n // 2 + 1
+        source = (y + jnp.where(n % 2 == 0, near, R // 2 - near)) % (R // 2)
+        slot = 4 * ((source // 2 - x + X) % X) + 2 * core + source % 2
+        pltpu.make_async_copy(inter_s.at[slot], inter_s.at[slot], grecv.at[source]).wait()
+        hand_on(slot)
+
+    others = inter_s.at[pl.ds(0, R // 2)]
+    pltpu.make_async_copy(others, others, frecv).wait()
     inter_out[...] = inter_s[...]
     flag_out[...] = inter_s[3].astype(F32)[8:16, 0:128]
 
     sent = pk.at[pl.ds(0, Z - 1)]
     pltpu.make_async_copy(sent, sent, zsend).wait()
-    sent = gbuf.at[pl.ds(0, Z * (X - 1))]
+    sent = gbuf.at[pl.ds(0, X - 1)]
     pltpu.make_async_copy(sent, sent, xsend).wait()
-    sent = part.at[pl.ds(0, R - 1)]
-    pltpu.make_async_copy(sent, sent, rsend).wait()
-    sent = inter_s.at[pl.ds(0, R - 1)]
+    swap.wait_send()
+    sent = inter_s.at[pl.ds(0, R // 2 - 1)]
     pltpu.make_async_copy(sent, sent, gsend).wait()
+    pltpu.make_async_copy(others, others, fsend).wait()
 
 
 def exchange(amplitudes, occ_energy, vir_energy, occ_irrep, vir_irrep, factors):
@@ -324,15 +399,20 @@
             pltpu.VMEM((OCC, WIDTH, NAUX), BF16),
             pltpu.VMEM((FOLD, 256), F32),
             pltpu.VMEM((Z, MAIN, 256), BF16),
-            pltpu.VMEM((X * Z, MAIN, 256), BF16),
-            pltpu.VMEM((R, MAIN, WINDOW), BF16),
-            pltpu.VMEM((R, MAIN, WINDOW), BF16),
+            pltpu.VMEM((X, Z, MAIN, 256), BF16),
+            pltpu.VMEM((GROUPS, MAIN, 256), I32),
+            pltpu.VMEM((2 * X, PAIRS, MAIN, 256), I32),
+            pltpu.VMEM((X * ROWS, COLS), BF16),
+            pltpu.VMEM((2, X, ROWS // 2, WINDOW), BF16),
+            pltpu.VMEM((X, ROWS // 2, WINDOW), BF16),
+            pltpu.VMEM((X, 2, MAIN, WINDOW), BF16),
+            pltpu.VMEM((R // 2, MAIN, WINDOW), BF16),
             pltpu.VMEM((R, MAIN, WINDOW), BF16),
             pltpu.VMEM((8, 128), F32),
-            dma((PAIRS + 1,)), dma, dma((Z,)), dma, dma((X,)), dma, dma, dma, dma,
+            dma((PAIRS + 1,)), dma, dma, dma, dma((X,)), dma, dma, dma, dma, dma, dma((R // 2,)), dma, dma,
         ],
         compiler_params=pltpu.CompilerParams(
-            collective_id=0, has_side_effects=True, vmem_limit_bytes=32 * 1024 * 1024
+            collective_id=0, has_side_effects=True, vmem_limit_bytes=62 * 1024 * 1024
         ),
         name="exchange",
     )(

time: 69.2 us -> 62.2 us (0.90)
  Pallas kernels: 53.2 us -> 45.5 us
    pallas_call x1, Pallas kernels: 50.4 us -> 42.8 us  [exchange(): pl.pallas_call(exchange_kernel, out_shape=[jax.ShapeDtypeStruct(*s) for s...]
where the time goes in v2:
time: 62.2 us; the launch traced here: 62 us
  Pallas kernels  45.5 us (73%)
  between operations  14.1 us (23%)
  local copies, waits for them, and re-layouts  2.4 us (4%)
    pallas_call x1, Pallas kernels, exchange(): pl.pallas_call(exchange_kernel, out_shape=[jax.ShapeDtypeStruct(*s) for s...  42.8 us
    pallas_call x1, Pallas kernels, finish(): pl.pallas_call(finish_kernel, out_shape=jax.ShapeDtypeStruct((OCC, OCC, S...  2.74 us

profile of v2, /device:TPU:1, one launch (start us, length us, event | category | flops | bytes accessed | tf_op | source)
XLA Modules:
  0.0 62.0 jit_solution(2050347641957331348)
XLA Ops:
  6.5 0.0 copy-start.2
  6.5 0.0 copy-start.3
  6.5 0.0 copy-start.4
  6.5 42.8 %exchange.1 = (bf16[4,64,1024]{2,1,0:T(8,128)(2,1)}, bf16[16,16,384]{2,1,0:T(8,128)(2,1)}, bf16[1024,384]{1,0:T(8,128)(2,1)}, s32[4,64,128]{2,1,0:T(8,128)}, f32...) custom-call(bf16[3,60,960]{2,1,0:T(8,128)(2,1)} %bitcast.30, ...), custom_call_target="tpu_custom_call" | custom-call | tf_op jit(solution)/shard_map/exchange/pallas_call | solution.py:392
  49.3 1.2 %slice.3 = f32[1,1]{1,0:T(1,128)} slice(f32[8,128]{1,0:T(8,128)} %get-tuple-element.59), slice={[7:8], [0:1]} | slice | bytes 8 | tf_op jit(solution)/shard_map/slice | solution.py:460
  51.1 0.0 copy-done.2
  51.2 0.0 copy-done.3
  51.2 0.0 copy-done.4
  51.2 2.8 %conditional.1 = (f32[12,20,12,60]{3,1,2,0:T(8,128)S(1)}) conditional(s32[]{:T(128)} %bitcast.14, (s32[12]{0:T(128)S(1)}, s32[960]{0:T(1024)}, bf16[3,960,60]{1,2,0:T(8,128)(2,1)S(1)}, bf16[12,60,2048]{2,1,0:T(8,128)(2,1)}, f32[12]{0:T(128)S(1)}, /*index=5*/f32[960]{0:T(1024)}) %tuple.24, (bf16[4,64,1024]{2,1,0:T(8,128)(2,1)}, ...), branch_computations={%region_0.2_spmd, %region_2.3_spmd} | conditional | flops 1417774336 | bytes 41846500 | solution.py:460
  51.2 2.7 %finish.1 = f32[12,12,20,60]{3,2,1,0:T(8,128)S(1)} custom-call(bf16[4,64,1024]{2,1,0:T(8,128)(2,1)} %get-tuple-element.42.m_ref, bf16[16,16,384]{2,1,0:T(8,128)(2,1)} %get-tuple-element.43.inter_ref, bf16[1024,384]{1,0:T(8,128)(2,1)} %get-tuple-element.44.ff_ref, s32[4,64,128]{2,1,0:T(8,128)} %get-tuple-element.45.row_lab, ...), custom_call_target="tpu_custom_call" | custom-call | tf_op jit(solution)/shard_map/cond/branch_1_fun/finish/pallas_call | solution.py:446
  53.9 0.0 copy-start.5
  53.9 1.2 %copy-done.5 = f32[12,20,12,60]{3,1,2,0:T(8,128)} copy-done((f32[12,20,12,60]{3,1,2,0:T(8,128)}, f32[12,20,12,60]{3,1,2,0:T(8,128)S(1)}, u32[]{:S(2)}) %copy-start.5) | copy-done | bytes 691224
Async XLA Ops:
  6.5 44.6 %copy-start.2 = (bf16[3,960,60]{1,2,0:T(8,128)(2,1)S(1)}, bf16[3,960,60]{1,2,0:T(8,128)(2,1)}, u32[]{:S(2)}) copy-start(bf16[3,960,60]{1,2,0:T(8,128)(2,1)} %param.8) | copy-start | bytes 1036804
  6.5 44.6 %copy-start.3 = (f32[12]{0:T(128)S(1)}, f32[12]{0:T(128)}, u32[]{:S(2)}) copy-start(f32[12]{0:T(128)} %occ_energy.1) | copy-start | bytes 148
  6.5 44.6 %copy-start.4 = (s32[12]{0:T(128)S(1)}, s32[12]{0:T(128)}, u32[]{:S(2)}) copy-start(s32[12]{0:T(128)} %occ_irrep.1) | copy-start | bytes 148
  53.9 1.2 %copy-start.5 = (f32[12,20,12,60]{3,1,2,0:T(8,128)}, f32[12,20,12,60]{3,1,2,0:T(8,128)S(1)}, u32[]{:S(2)}) copy-start(f32[12,20,12,60]{3,1,2,0:T(8,128)S(1)} %get-tuple-element.96) | copy-start | bytes 2073604

commit v3 on v2

--- a/solution.py
+++ b/solution.py
@@ -23,6 +23,16 @@
 F32, BF16, I32 = jnp.float32, jnp.bfloat16, jnp.int32
 
 
+def sum_over_rep(partial_value):
+    count = lax.axis_size("rep")
+    blocks = partial_value.reshape(count, -1, partial_value.shape[1])
+    blocks = lax.all_to_all(blocks, "rep", split_axis=0, concat_axis=0, tiled=True)
+    total = jnp.sum(blocks.astype(jnp.float32), axis=0).astype(jnp.bfloat16)
+    total = jnp.broadcast_to(total[None], blocks.shape)
+    total = lax.all_to_all(total, "rep", split_axis=0, concat_axis=0, tiled=True)
+    return total.reshape(partial_value.shape)
+
+
 def dense_path(amplitudes, occ_energy, vir_energy, occ_irrep, vir_irrep, factors):
     tile_count = lax.axis_size("tile")
     occ_count = occ_energy.shape[0]
@@ -34,7 +44,7 @@
     matrix = relaid.reshape(occ_count * first_width, occ_count * second_width)
     factor_rows = factors.reshape(occ_count * second_width, factors.shape[2])
     partial_value = jnp.dot(matrix, factor_rows, preferred_element_type=jnp.float32)
-    inter = lax.psum(partial_value.astype(jnp.bfloat16), "rep")
+    inter = sum_over_rep(partial_value.astype(jnp.bfloat16))
     cycle = jnp.einsum("mq,nq->mn", inter, factor_rows, preferred_element_type=jnp.float32)
     cycle = cycle.reshape(occ_count, first_width, occ_count, second_width)
     tile_start = lax.axis_index("tile") * first_width

time: 62.2 us -> 48.8 us (0.78)
  between operations: 14.1 us -> 0.7 us
where the time goes in v3:
time: 48.8 us; the launch traced here: 48.6 us
  Pallas kernels  45.5 us (93%)
  local copies, waits for them, and re-layouts  2.4 us (5%)
  between operations  0.7 us (1%)
    pallas_call x1, Pallas kernels, exchange(): pl.pallas_call(exchange_kernel, out_shape=[jax.ShapeDtypeStruct(*s) for s...  42.7 us
    pallas_call x1, Pallas kernels, finish(): pl.pallas_call(finish_kernel, out_shape=jax.ShapeDtypeStruct((OCC, OCC, S...  2.74 us
    unnamed x8, local copies, waits for them, and re-layouts  1.21 us
    slice x1, local copies, waits for them, and re-layouts, per_device(): flag[7, 0] == 0.0  1.19 us

profile of v3, /device:TPU:1, one launch (start us, length us, event | category | flops | bytes accessed | tf_op | source)
XLA Modules:
  0.0 48.6 jit_solution(9365436060902227222)
XLA Ops:
  0.0 0.0 copy-start.2
  0.0 0.0 copy-start.3
  0.0 0.0 copy-start.4
  0.0 42.7 %exchange.1 = (bf16[4,64,1024]{2,1,0:T(8,128)(2,1)}, bf16[16,16,384]{2,1,0:T(8,128)(2,1)}, bf16[1024,384]{1,0:T(8,128)(2,1)}, s32[4,64,128]{2,1,0:T(8,128)}, f32...) custom-call(bf16[3,60,960]{2,1,0:T(8,128)(2,1)} %bitcast.28, ...), custom_call_target="tpu_custom_call" | custom-call | tf_op jit(solution)/shard_map/exchange/pallas_call | solution.py:402
  42.8 1.2 %slice.3 = f32[1,1]{1,0:T(1,128)} slice(f32[8,128]{1,0:T(8,128)} %get-tuple-element.59), slice={[7:8], [0:1]} | slice | bytes 8 | tf_op jit(solution)/shard_map/slice | solution.py:470
  44.6 0.0 copy-done.2
  44.6 0.0 copy-done.3
  44.6 0.0 copy-done.4
  44.6 2.8 %conditional.1 = (f32[12,20,12,60]{3,1,2,0:T(8,128)S(1)}) conditional(s32[]{:T(128)} %bitcast.13, (s32[12]{0:T(128)S(1)}, s32[960]{0:T(1024)}, bf16[3,960,60]{1,2,0:T(8,128)(2,1)S(1)}, bf16[12,60,2048]{2,1,0:T(8,128)(2,1)}, f32[12]{0:T(128)S(1)}, /*index=5*/f32[960]{0:T(1024)}) %tuple.22, (bf16[4,64,1024]{2,1,0:T(8,128)(2,1)}, ...), branch_computations={%region_0.2_spmd, %region_2.3_spmd} | conditional | flops 1417743616 | bytes 44656348 | solution.py:470
  44.6 2.7 %finish.1 = f32[12,12,20,60]{3,2,1,0:T(8,128)S(1)} custom-call(bf16[4,64,1024]{2,1,0:T(8,128)(2,1)} %get-tuple-element.42.m_ref, bf16[16,16,384]{2,1,0:T(8,128)(2,1)} %get-tuple-element.43.inter_ref, bf16[1024,384]{1,0:T(8,128)(2,1)} %get-tuple-element.44.ff_ref, s32[4,64,128]{2,1,0:T(8,128)} %get-tuple-element.45.row_lab, ...), custom_call_target="tpu_custom_call" | custom-call | tf_op jit(solution)/shard_map/cond/branch_1_fun/finish/pallas_call | solution.py:456
  47.4 0.0 copy-start.5
  47.4 1.2 %copy-done.5 = f32[12,20,12,60]{3,1,2,0:T(8,128)} copy-done((f32[12,20,12,60]{3,1,2,0:T(8,128)}, f32[12,20,12,60]{3,1,2,0:T(8,128)S(1)}, u32[]{:S(2)}) %copy-start.5) | copy-done | bytes 691224
Async XLA Ops:
  0.0 44.6 %copy-start.2 = (bf16[3,960,60]{1,2,0:T(8,128)(2,1)S(1)}, bf16[3,960,60]{1,2,0:T(8,128)(2,1)}, u32[]{:S(2)}) copy-start(bf16[3,960,60]{1,2,0:T(8,128)(2,1)} %param.8) | copy-start | bytes 1036804
  0.0 44.6 %copy-start.3 = (f32[12]{0:T(128)S(1)}, f32[12]{0:T(128)}, u32[]{:S(2)}) copy-start(f32[12]{0:T(128)} %occ_energy.1) | copy-start | bytes 148
  0.0 44.6 %copy-start.4 = (s32[12]{0:T(128)S(1)}, s32[12]{0:T(128)}, u32[]{:S(2)}) copy-start(s32[12]{0:T(128)} %occ_irrep.1) | copy-start | bytes 148
  47.4 1.2 %copy-start.5 = (f32[12,20,12,60]{3,1,2,0:T(8,128)}, f32[12,20,12,60]{3,1,2,0:T(8,128)S(1)}, u32[]{:S(2)}) copy-start(f32[12,20,12,60]{3,1,2,0:T(8,128)S(1)} %get-tuple-element.94) | copy-start | bytes 2073604

commit v4 on v3

--- a/solution.py
+++ b/solution.py
@@ -97,10 +97,11 @@
 
 
 def exchange_kernel(
-    amp_hbm, fac_hbm, vir_irrep, vir_energy, occ_irrep, occ_energy,
-    m_out, inter_out, ff_out, row_lab, row_en, col_lab, col_occ, col_vir, flag_out,
-    amp_v, fac_v, pkf, pk, gbuf, bcol, brow, ms, part, cbuf, send, rsbuf, inter_s, flag_s,
-    load_sem, zsend, zrecv, xsend, xrecv, csend, crecv, rsend, rrecv, gsend, grecv, fsend, frecv,
+    amp_hbm, fac_hbm, vir_irrep_hbm, vir_energy_hbm, occ_irrep_hbm, occ_energy_hbm,
+    m_hbm, inter_hbm, ff_hbm, rows_hbm, cols_hbm, flag_out,
+    amp_v, fac_v, vir_irrep, vir_energy, occ_irrep, occ_energy, m_out, ff_out, rows_out, cols_out,
+    pkf, pk, gbuf, bcol, brow, ms, part, cbuf, send, rsbuf, inter_s, flag_s,
+    load_sem, out_sem, zsend, zrecv, xsend, xrecv, csend, crecv, rsend, rrecv, gsend, grecv, fsend, frecv,
 ):
     t = lax.axis_index("tile")
     r = lax.axis_index("rep")
@@ -112,9 +113,13 @@
 
     loads = [pltpu.make_async_copy(amp_hbm.at[j], amp_v.at[j], load_sem.at[j]) for j in range(PAIRS)]
     loads.append(pltpu.make_async_copy(fac_hbm, fac_v, load_sem.at[PAIRS]))
-    for copy in loads:
-        copy.start()
-
+    small = [
+        (vir_irrep_hbm, vir_irrep), (vir_energy_hbm, vir_energy),
+        (occ_irrep_hbm, occ_irrep), (occ_energy_hbm, occ_energy),
+    ]
+    small = [pltpu.make_async_copy(a, b, load_sem.at[PAIRS + 1 + n]) for n, (a, b) in enumerate(small)]
+    saves = [(ff_out, ff_hbm), (rows_out, rows_hbm), (cols_out, cols_hbm), (m_out, m_hbm), (inter_s, inter_hbm)]
+    saves = [pltpu.make_async_copy(a, b, out_sem.at[n]) for n, (a, b) in enumerate(saves)]
     barrier = pltpu.get_barrier_semaphore()
 
     def z_peer(n):
@@ -124,6 +129,9 @@
     @pl.loop(0, Z - 1)
     def _(n):
         pl.semaphore_signal(barrier, inc=1, device_id=(x * Z + z_peer(n), r))
+
+    for copy in loads[:PAIRS] + small + loads[PAIRS:]:
+        copy.start()
 
     def reducer(d, h):
         return 2 * (2 * ((x + d) % X) + h) + core
@@ -181,6 +189,8 @@
 
     gbuf[x, z] = pk[z]
 
+    for copy in small:
+        copy.wait()
     vlane = lax.broadcasted_iota(I32, (24, X * FOLD), 1)
     vsub = lax.broadcasted_iota(I32, (24, X * FOLD), 0)
     virs = vir_irrep[...].astype(F32)
@@ -197,15 +207,15 @@
     for i in range(OCC):
         n, i3 = i // PAIRS, i % PAIRS
         brow[X + n, i3] = block_rows(va_lab, occ_irrep[i])
-        lab = jnp.broadcast_to(jnp.bitwise_xor(va_lab, occ_irrep[i]), (24, 128))
+        lab = jnp.broadcast_to(jnp.bitwise_xor(va_lab, occ_irrep[i]).astype(F32), (24, 128))
         en = jnp.broadcast_to(occ_energy[i] - va_en, (24, 128))
-        row_lab[n, MAIN * i3 : MAIN * (i3 + 1), :] = lab[:MAIN]
-        row_lab[n, MAIN * PAIRS + REM * i3 : MAIN * PAIRS + REM * (i3 + 1), :] = lab[MAIN:SLAB]
-        row_en[n, MAIN * i3 : MAIN * (i3 + 1), :] = en[:MAIN]
-        row_en[n, MAIN * PAIRS + REM * i3 : MAIN * PAIRS + REM * (i3 + 1), :] = en[MAIN:SLAB]
-    for n in range(X):
-        row_lab[n, ROWS - REM : ROWS, :] = jnp.full((REM, 128), -1, I32)
-        row_en[n, ROWS - REM : ROWS, :] = jnp.zeros((REM, 128), F32)
+        rows_out[0, n, MAIN * i3 : MAIN * (i3 + 1), :] = lab[:MAIN]
+        rows_out[0, n, MAIN * PAIRS + REM * i3 : MAIN * PAIRS + REM * (i3 + 1), :] = lab[MAIN:SLAB]
+        rows_out[1, n, MAIN * i3 : MAIN * (i3 + 1), :] = en[:MAIN]
+        rows_out[1, n, MAIN * PAIRS + REM * i3 : MAIN * PAIRS + REM * (i3 + 1), :] = en[MAIN:SLAB]
+    for n in range(X):
+        rows_out[0, n, ROWS - REM : ROWS, :] = jnp.full((REM, 128), -1.0, F32)
+        rows_out[1, n, ROWS - REM : ROWS, :] = jnp.zeros((REM, 128), F32)
 
     pad = jnp.zeros((8, 1024 - X * FOLD), F32)
     shift = (1024 - WIDTH * r) % 1024
@@ -228,9 +238,9 @@
             cols = slice(256 * g + 128 * h, 256 * g + 128 * h + 128)
             lab = jnp.bitwise_xor(vb_lab, jnp.where(lane8 < 64, occ_irrep[first], occ_irrep[second]))
             lab = jnp.where(half < WIDTH, lab, -2)
-            col_lab[:, cols] = jnp.where((lane8 < 64) | (h == 0), lab, -2)
-            col_occ[:, cols] = jnp.where(lane8 < 64, occ_energy[first], occ_energy[second])
-            col_vir[:, cols] = vb_en
+            cols_out[0, :, cols] = jnp.where((lane8 < 64) | (h == 0), lab, -2).astype(F32)
+            cols_out[1, :, cols] = jnp.where(lane8 < 64, occ_energy[first], occ_energy[second])
+            cols_out[2, :, cols] = vb_en
             lab = jnp.concatenate([lab, lab], axis=0)
             if h == 1:
                 occ = [occ_irrep[PAIRS * g + j] for j in range(PAIRS)]
@@ -238,6 +248,9 @@
                 rem = jnp.where((lane_iota(MAIN) & 63) < WIDTH, jnp.bitwise_xor(vb_lab16, occ), -2)
                 lab = jnp.where(lane_iota(MAIN) < 64, lab, rem)
             bcol[g, :, 128 * h : 128 * h + 128] = lab
+
+    saves[1].start()
+    saves[2].start()
 
     loads[PAIRS].wait()
     zero4 = jnp.zeros((64 - WIDTH, WINDOW), F32)
@@ -253,6 +266,7 @@
         total = total + jnp.concatenate([tail, jnp.zeros((WIDTH, WINDOW - NAUX + last), F32)], axis=1)
         ff_out[base : base + 64, :] = jnp.concatenate([total, zero4], axis=0).astype(BF16)
 
+    saves[0].start()
     vlane8 = lax.broadcasted_iota(I32, (8, X * FOLD), 1)
     vsub8 = lax.broadcasted_iota(I32, (8, X * FOLD), 0)
     first_lab = jnp.sum(
@@ -360,6 +374,8 @@
             m_out.at[xs], [gbuf[xs, n] for n in range(Z)], [brow[X + xs, i3] for i3 in range(PAIRS)], cols
         )
 
+    saves[3].start()
+
     @pl.loop(0, R // 2 - 1)
     def _(n):
         near = n // 2 + 1
@@ -370,8 +386,8 @@
 
     others = inter_s.at[pl.ds(0, R // 2)]
     pltpu.make_async_copy(others, others, frecv).wait()
-    inter_out[...] = inter_s[...]
-    flag_out[...] = inter_s[3].astype(F32)[8:16, 0:128]
+    saves[4].start()
+    flag_out[0] = jnp.max(inter_s[3].astype(F32)[15:16, 0:128])
 
     sent = pk.at[pl.ds(0, Z - 1)]
     pltpu.make_async_copy(sent, sent, zsend).wait()
@@ -381,32 +397,37 @@
     sent = inter_s.at[pl.ds(0, R // 2 - 1)]
     pltpu.make_async_copy(sent, sent, gsend).wait()
     pltpu.make_async_copy(others, others, fsend).wait()
+    for copy in saves:
+        copy.wait()
 
 
 def exchange(amplitudes, occ_energy, vir_energy, occ_irrep, vir_irrep, factors):
-    vmem = pl.BlockSpec(memory_space=pltpu.VMEM)
+    hbm = pl.BlockSpec(memory_space=pl.ANY)
     smem = pl.BlockSpec(memory_space=pltpu.SMEM)
-    hbm = pl.BlockSpec(memory_space=pl.ANY)
     shapes = [
         ((X, ROWS, COLS), BF16),
         ((R, MAIN, WINDOW), BF16),
         ((COLS, WINDOW), BF16),
-        ((X, ROWS, 128), I32),
-        ((X, ROWS, 128), F32),
-        ((8, COLS), I32),
-        ((8, COLS), F32),
-        ((8, COLS), F32),
-        ((8, 128), F32),
+        ((2, X, ROWS, 128), F32),
+        ((3, 8, COLS), F32),
     ]
     dma = pltpu.SemaphoreType.DMA
     return pl.pallas_call(
         exchange_kernel,
-        out_shape=[jax.ShapeDtypeStruct(*s) for s in shapes],
-        in_specs=[hbm, hbm, vmem, vmem, smem, smem],
-        out_specs=[vmem] * len(shapes),
+        out_shape=[jax.ShapeDtypeStruct(*s) for s in shapes] + [jax.ShapeDtypeStruct((1,), F32)],
+        in_specs=[hbm] * 6,
+        out_specs=[hbm] * 5 + [smem],
         scratch_shapes=[
             pltpu.VMEM((PAIRS, WIDTH, X * FOLD), BF16),
             pltpu.VMEM((OCC, WIDTH, NAUX), BF16),
+            pltpu.VMEM((1, X * FOLD), I32),
+            pltpu.VMEM((1, X * FOLD), F32),
+            pltpu.SMEM((OCC,), I32),
+            pltpu.SMEM((OCC,), F32),
+            pltpu.VMEM((X, ROWS, COLS), BF16),
+            pltpu.VMEM((COLS, WINDOW), BF16),
+            pltpu.VMEM((2, X, ROWS, 128), F32),
+            pltpu.VMEM((3, 8, COLS), F32),
             pltpu.VMEM((FOLD, 256), F32),
             pltpu.VMEM((Z, MAIN, 256), BF16),
             pltpu.VMEM((X, Z, MAIN, 256), BF16),
@@ -419,7 +440,7 @@
             pltpu.VMEM((R // 2, MAIN, WINDOW), BF16),
             pltpu.VMEM((R, MAIN, WINDOW), BF16),
             pltpu.VMEM((8, 128), F32),
-            dma((PAIRS + 1,)), dma, dma, dma, dma((X,)), dma, dma, dma, dma, dma, dma((R // 2,)), dma, dma,
+            dma((PAIRS + 5,)), dma((5,)), dma, dma, dma, dma((X,)), dma, dma, dma, dma, dma, dma((R // 2,)), dma, dma,
         ],
         compiler_params=pltpu.CompilerParams(
             collective_id=0, has_side_effects=True, vmem_limit_bytes=62 * 1024 * 1024
@@ -431,17 +452,17 @@
     )
 
 
-def finish_kernel(m_ref, inter_ref, ff_ref, row_lab, row_en, col_lab, col_occ, col_vir, out, res):
+def finish_kernel(m_ref, inter_ref, ff_ref, rows_ref, cols_ref, out_hbm, out, res, sem):
     for n in range(X):
         inter = jnp.concatenate([inter_ref[4 * n + c] for c in range(4)], axis=0)
         cycle = lax.dot_general(inter, ff_ref[...], (((1,), (1,)), ((), ())), preferred_element_type=F32)
+        rlab = jnp.concatenate([rows_ref[0, n]] * 2, axis=1)
+        ren = jnp.concatenate([rows_ref[1, n]] * 2, axis=1)
         for g in range(GROUPS):
             cols = slice(256 * g, 256 * (g + 1))
-            rlab = jnp.concatenate([row_lab[n]] * 2, axis=1)
-            ren = jnp.concatenate([row_en[n]] * 2, axis=1)
-            denom = ren + col_occ[0:1, cols] - col_vir[0:1, cols]
+            denom = ren + cols_ref[1, 0:1, cols] - cols_ref[2, 0:1, cols]
             value = m_ref[n, :, cols].astype(F32) + cycle[:, cols] / denom
-            res[:, cols] = jnp.where(rlab == col_lab[0:1, cols], value, 0.0)
+            res[:, cols] = jnp.where(rlab == cols_ref[0, 0:1, cols], value, 0.0)
         for i3 in range(PAIRS):
             i = PAIRS * n + i3
             for j in range(OCC):
@@ -449,6 +470,11 @@
                 out[i, j, 0:MAIN, :] = res[MAIN * i3 : MAIN * (i3 + 1), base : base + WIDTH]
                 rem = MAIN * PAIRS + REM * i3
                 out[i, j, MAIN:SLAB, :] = res[rem : rem + REM, base : base + WIDTH]
+        done = pl.ds(PAIRS * n, PAIRS)
+        pltpu.make_async_copy(out.at[done], out_hbm.at[done], sem.at[n]).start()
+    for n in range(X):
+        done = pl.ds(PAIRS * n, PAIRS)
+        pltpu.make_async_copy(out.at[done], out_hbm.at[done], sem.at[n]).wait()
 
 
 def finish(*operands):
@@ -456,10 +482,14 @@
     out = pl.pallas_call(
         finish_kernel,
         out_shape=jax.ShapeDtypeStruct((OCC, OCC, SLAB, WIDTH), F32),
-        in_specs=[vmem] * 8,
-        out_specs=vmem,
-        scratch_shapes=[pltpu.VMEM((ROWS, COLS), F32)],
-        compiler_params=pltpu.CompilerParams(vmem_limit_bytes=32 * 1024 * 1024),
+        in_specs=[vmem] * 5,
+        out_specs=pl.BlockSpec(memory_space=pltpu.HBM),
+        scratch_shapes=[
+            pltpu.VMEM((OCC, OCC, SLAB, WIDTH), F32),
+            pltpu.VMEM((ROWS, COLS), F32),
+            pltpu.SemaphoreType.DMA((X,)),
+        ],
+        compiler_params=pltpu.CompilerParams(vmem_limit_bytes=62 * 1024 * 1024),
         name="finish",
     )(*operands)
     return out.transpose(0, 2, 1, 3)
@@ -467,7 +497,7 @@
 
 def per_device(*arguments):
     *operands, flag = exchange(*arguments)
-    return lax.cond(flag[7, 0] == 0.0, lambda: finish(*operands), lambda: dense_path(*arguments))
+    return lax.cond(flag[0] == 0.0, lambda: finish(*operands), lambda: dense_path(*arguments))
 
 
 def solution(mesh):

time: 48.8 us -> 46.3 us (0.949)
  local copies, waits for them, and re-layouts: 2.4 us -> 0.01 us
    unnamed x8 -> x6, local copies, waits for them, and re-layouts: 1.21 us -> 0.01 us
    slice x1 -> x0, local copies, waits for them, and re-layouts: 1.19 us -> none  [per_device(): flag[7, 0] == 0.0]
    pallas_call x1, Pallas kernels: 42.7 us -> 41.9 us  [exchange(): pl.pallas_call(exchange_kernel, out_shape=[jax.ShapeDtypeStruct(*s) for s...]
    pallas_call x1, Pallas kernels: 2.74 us -> 3.49 us  [finish(): pl.pallas_call(finish_kernel, out_shape=jax.ShapeDtypeStruct((OCC, OCC, S...]
where the time goes in v4:
time: 46.3 us; the launch traced here: 46.1 us
  Pallas kernels  45.4 us (98%)
  between operations  0.67 us (1%)
    pallas_call x1, Pallas kernels, exchange(): pl.pallas_call(exchange_kernel, out_shape=[jax.ShapeDtypeStruct(*s) for s...  41.9 us
    pallas_call x1, Pallas kernels, finish(): pl.pallas_call(finish_kernel, out_shape=jax.ShapeDtypeStruct((OCC, OCC, S...  3.49 us

profile of v4, /device:TPU:1, one launch (start us, length us, event | category | flops | bytes accessed | tf_op | source)
XLA Modules:
  0.0 46.1 jit_solution(12767135886315387881)
XLA Ops:
  0.0 0.0 copy-start.2
  0.0 0.0 copy-start.3
  0.0 0.0 copy-start.4
  0.0 41.9 %exchange.1 = (bf16[4,64,1024]{2,1,0:T(8,128)(2,1)}, bf16[16,16,384]{2,1,0:T(8,128)(2,1)}, bf16[1024,384]{1,0:T(8,128)(2,1)}, f32[2,4,64,128]{3,2,1,0:T(8,128)}, f32[3,8,1024]{2,1,0:T(8,128)}, /*index=5*/f32[1]{0:T(128)}) custom-call(bf16[3,60,960]{2,1,0:T(8,128)(2,1)} %bitcast.28, bf16[12,60,2048]{2,1,0:T(8,128)(2,1)} %fac_hbm.1, s32[1,960]{1,0:T(1,128)} %bitcast.29, ...), custom_call_target="tpu_custom_call" | custom-call | tf_op jit(solution)/shard_map/exchange/pallas_call | solution.py:415
  42.6 0.0 copy-done.2
  42.6 0.0 copy-done.3
  42.6 0.0 copy-done.4
  42.6 3.5 %conditional.1 = (f32[12,20,12,60]{3,1,2,0:T(8,128)}) conditional(s32[]{:T(128)} %bitcast.13, (s32[12]{0:T(128)S(1)}, s32[960]{0:T(1024)}, bf16[3,960,60]{1,2,0:T(8,128)(2,1)S(1)}, bf16[12,60,2048]{2,1,0:T(8,128)(2,1)}, f32[12]{0:T(128)S(1)}, /*index=5*/f32[960]{0:T(1024)}) %tuple.22, (bf16[4,64,1024]{2,1,0:T(8,128)(2,1)}, ...), branch_computations={%region_0.2_spmd, %region_2.3_spmd} | conditional | flops 1417743616 | bytes 44656348 | solution.py:500
  42.6 3.5 %finish.1 = f32[12,12,20,60]{3,2,1,0:T(8,128)} custom-call(bf16[4,64,1024]{2,1,0:T(8,128)(2,1)} %get-tuple-element.36.m_ref, bf16[16,16,384]{2,1,0:T(8,128)(2,1)} %get-tuple-element.37.inter_ref, bf16[1024,384]{1,0:T(8,128)(2,1)} %get-tuple-element.38.ff_ref, f32[2,4,64,128]{3,2,1,0:T(8,128)} %get-tuple-element.39.rows_ref, ...), custom_call_target="tpu_custom_call" | custom-call | tf_op jit(solution)/shard_map/cond/branch_1_fun/finish/pallas_call | solution.py:482
Async XLA Ops:
  0.0 42.6 %copy-start.2 = (bf16[3,960,60]{1,2,0:T(8,128)(2,1)S(1)}, bf16[3,960,60]{1,2,0:T(8,128)(2,1)}, u32[]{:S(2)}) copy-start(bf16[3,960,60]{1,2,0:T(8,128)(2,1)} %param.8) | copy-start | bytes 1036804
  0.0 42.6 %copy-start.3 = (f32[12]{0:T(128)S(1)}, f32[12]{0:T(128)}, u32[]{:S(2)}) copy-start(f32[12]{0:T(128)} %occ_energy_hbm.1) | copy-start | bytes 148
  0.0 42.6 %copy-start.4 = (s32[12]{0:T(128)S(1)}, s32[12]{0:T(128)}, u32[]{:S(2)}) copy-start(s32[12]{0:T(128)} %occ_irrep_hbm.1) | copy-start | bytes 148

commit v5 on v4

--- a/solution.py
+++ b/solution.py
@@ -98,10 +98,9 @@
 
 def exchange_kernel(
     amp_hbm, fac_hbm, vir_irrep_hbm, vir_energy_hbm, occ_irrep_hbm, occ_energy_hbm,
-    m_hbm, inter_hbm, ff_hbm, rows_hbm, cols_hbm, flag_out,
-    amp_v, fac_v, vir_irrep, vir_energy, occ_irrep, occ_energy, m_out, ff_out, rows_out, cols_out,
-    pkf, pk, gbuf, bcol, brow, ms, part, cbuf, send, rsbuf, inter_s, flag_s,
-    load_sem, out_sem, zsend, zrecv, xsend, xrecv, csend, crecv, rsend, rrecv, gsend, grecv, fsend, frecv,
+    m_out, inter_out, ff_out, rows_out, cols_out, flag_out,
+    amp_v, fac_v, vir_irrep, vir_energy, occ_irrep, occ_energy, pkf, pk, gbuf, bcol, brow, ms, part, cbuf, send, rsbuf, inter_s, flag_s,
+    load_sem, zsend, zrecv, xsend, xrecv, csend, crecv, rsend, rrecv, gsend, grecv, fsend, frecv,
 ):
     t = lax.axis_index("tile")
     r = lax.axis_index("rep")
@@ -118,8 +117,6 @@
         (occ_irrep_hbm, occ_irrep), (occ_energy_hbm, occ_energy),
     ]
     small = [pltpu.make_async_copy(a, b, load_sem.at[PAIRS + 1 + n]) for n, (a, b) in enumerate(small)]
-    saves = [(ff_out, ff_hbm), (rows_out, rows_hbm), (cols_out, cols_hbm), (m_out, m_hbm), (inter_s, inter_hbm)]
-    saves = [pltpu.make_async_copy(a, b, out_sem.at[n]) for n, (a, b) in enumerate(saves)]
     barrier = pltpu.get_barrier_semaphore()
 
     def z_peer(n):
@@ -249,8 +246,6 @@
                 lab = jnp.where(lane_iota(MAIN) < 64, lab, rem)
             bcol[g, :, 128 * h : 128 * h + 128] = lab
 
-    saves[1].start()
-    saves[2].start()
 
     loads[PAIRS].wait()
     zero4 = jnp.zeros((64 - WIDTH, WINDOW), F32)
@@ -266,7 +261,6 @@
         total = total + jnp.concatenate([tail, jnp.zeros((WIDTH, WINDOW - NAUX + last), F32)], axis=1)
         ff_out[base : base + 64, :] = jnp.concatenate([total, zero4], axis=0).astype(BF16)
 
-    saves[0].start()
     vlane8 = lax.broadcasted_iota(I32, (8, X * FOLD), 1)
     vsub8 = lax.broadcasted_iota(I32, (8, X * FOLD), 0)
     first_lab = jnp.sum(
@@ -374,8 +368,6 @@
             m_out.at[xs], [gbuf[xs, n] for n in range(Z)], [brow[X + xs, i3] for i3 in range(PAIRS)], cols
         )
 
-    saves[3].start()
-
     @pl.loop(0, R // 2 - 1)
     def _(n):
         near = n // 2 + 1
@@ -386,7 +378,7 @@
 
     others = inter_s.at[pl.ds(0, R // 2)]
     pltpu.make_async_copy(others, others, frecv).wait()
-    saves[4].start()
+    inter_out[...] = inter_s[...]
     flag_out[0] = jnp.max(inter_s[3].astype(F32)[15:16, 0:128])
 
     sent = pk.at[pl.ds(0, Z - 1)]
@@ -397,8 +389,6 @@
     sent = inter_s.at[pl.ds(0, R // 2 - 1)]
     pltpu.make_async_copy(sent, sent, gsend).wait()
     pltpu.make_async_copy(others, others, fsend).wait()
-    for copy in saves:
-        copy.wait()
 
 
 def exchange(amplitudes, occ_energy, vir_energy, occ_irrep, vir_irrep, factors):
@@ -414,9 +404,9 @@
     dma = pltpu.SemaphoreType.DMA
     return pl.pallas_call(
         exchange_kernel,
-        out_shape=[jax.ShapeDtypeStruct(*s) for s in shapes] + [jax.ShapeDtypeStruct((1,), F32)],
+        out_shape=[pltpu.VMEM(*s) for s in shapes] + [jax.ShapeDtypeStruct((1,), F32)],
         in_specs=[hbm] * 6,
-        out_specs=[hbm] * 5 + [smem],
+        out_specs=[pl.BlockSpec(memory_space=pltpu.VMEM)] * 5 + [smem],
         scratch_shapes=[
             pltpu.VMEM((PAIRS, WIDTH, X * FOLD), BF16),
             pltpu.VMEM((OCC, WIDTH, NAUX), BF16),
@@ -424,10 +414,6 @@
             pltpu.VMEM((1, X * FOLD), F32),
             pltpu.SMEM((OCC,), I32),
             pltpu.SMEM((OCC,), F32),
-            pltpu.VMEM((X, ROWS, COLS), BF16),
-            pltpu.VMEM((COLS, WINDOW), BF16),
-            pltpu.VMEM((2, X, ROWS, 128), F32),
-            pltpu.VMEM((3, 8, COLS), F32),
             pltpu.VMEM((FOLD, 256), F32),
             pltpu.VMEM((Z, MAIN, 256), BF16),
             pltpu.VMEM((X, Z, MAIN, 256), BF16),
@@ -440,10 +426,10 @@
             pltpu.VMEM((R // 2, MAIN, WINDOW), BF16),
             pltpu.VMEM((R, MAIN, WINDOW), BF16),
             pltpu.VMEM((8, 128), F32),
-            dma((PAIRS + 5,)), dma((5,)), dma, dma, dma, dma((X,)), dma, dma, dma, dma, dma, dma((R // 2,)), dma, dma,
+            dma((PAIRS + 5,)), dma, dma, dma, dma((X,)), dma, dma, dma, dma, dma, dma((R // 2,)), dma, dma,
         ],
         compiler_params=pltpu.CompilerParams(
-            collective_id=0, has_side_effects=True, vmem_limit_bytes=62 * 1024 * 1024
+            collective_id=0, has_side_effects=True, vmem_limit_bytes=24 * 1024 * 1024
         ),
         name="exchange",
     )(
@@ -481,7 +467,7 @@
     vmem = pl.BlockSpec(memory_space=pltpu.VMEM)
     out = pl.pallas_call(
         finish_kernel,
-        out_shape=jax.ShapeDtypeStruct((OCC, OCC, SLAB, WIDTH), F32),
+        out_shape=pltpu.HBM((OCC, OCC, SLAB, WIDTH), F32),
         in_specs=[vmem] * 5,
         out_specs=pl.BlockSpec(memory_space=pltpu.HBM),
         scratch_shapes=[
@@ -489,7 +475,7 @@
             pltpu.VMEM((ROWS, COLS), F32),
             pltpu.SemaphoreType.DMA((X,)),
         ],
-        compiler_params=pltpu.CompilerParams(vmem_limit_bytes=62 * 1024 * 1024),
+        compiler_params=pltpu.CompilerParams(vmem_limit_bytes=24 * 1024 * 1024),
         name="finish",
     )(*operands)
     return out.transpose(0, 2, 1, 3)

time: 46.3 us -> 44.2 us (0.955)
  Pallas kernels: 45.4 us -> 43.4 us
    pallas_call x2, Pallas kernels: 45.4 us -> 43.4 us  [the longest x1 41.3 us: exchange(): pl.pallas_call(exchange_kernel, out_shape=[pltpu.VMEM(*s) for s in shapes...]
where the time goes in v5:
time: 44.2 us; the launch traced here: 44.1 us
  Pallas kernels  43.4 us (98%)
  between operations  0.67 us (2%)
    pallas_call x1, Pallas kernels, exchange(): pl.pallas_call(exchange_kernel, out_shape=[pltpu.VMEM(*s) for s in shapes...  41.3 us
    pallas_call x1, Pallas kernels, finish(): pl.pallas_call(finish_kernel, out_shape=pltpu.HBM((OCC, OCC, SLAB, WIDTH)...  2.01 us

profile of v5, /device:TPU:1, one launch (start us, length us, event | category | flops | bytes accessed | tf_op | source)
XLA Modules:
  0.0 44.1 jit_solution(11486897654488946641)
XLA Ops:
  0.0 0.0 copy-start.2
  0.0 0.0 copy-start.3
  0.0 0.0 copy-start.4
  0.0 41.3 %exchange.1 = (bf16[4,64,1024]{2,1,0:T(8,128)(2,1)S(1)}, bf16[16,16,384]{2,1,0:T(8,128)(2,1)S(1)}, bf16[1024,384]{1,0:T(8,128)(2,1)S(1)}, f32[2,4,64,128]{3,2,1,...) custom-call(bf16[3,60,960]{2,1,0:T(8,128)(2,1)} %bitcast.28, bf16[12,60,2048]{2,1,0:T(8,128)(2,1)} %fac_hbm.1, ...), custom_call_target="tpu_custom_call" | custom-call | tf_op jit(solution)/shard_map/exchange/pallas_call | solution.py:405
  42.0 0.0 copy-done.2
  42.0 0.0 copy-done.3
  42.0 0.0 copy-done.4
  42.0 2.0 %conditional.1 = (f32[12,20,12,60]{3,1,2,0:T(8,128)}) conditional(s32[]{:T(128)} %bitcast.13, (s32[12]{0:T(128)S(1)}, s32[960]{0:T(1024)}, bf16[3,960,60]{1,2,0:T(8,128)(2,1)S(1)}, bf16[12,60,2048]{2,1,0:T(8,128)(2,1)}, f32[12]{0:T(128)S(1)}, /*index=5*/f32[960]{0:T(1024)}) %tuple.22, (bf16[4,64,1024]{2,1,0:T(8,128)(2,1)S(1)}, ...), branch_computations={%region_0.2_spmd, %region_2.3_spmd} | conditional | flops 1417743616 | bytes 34242272 | solution.py:486
  42.0 2.0 %finish.1 = f32[12,12,20,60]{3,2,1,0:T(8,128)} custom-call(bf16[4,64,1024]{2,1,0:T(8,128)(2,1)S(1)} %get-tuple-element.36.m_ref, bf16[16,16,384]{2,1,0:T(8,128)(2,1)S(1)} %get-tuple-element.37.inter_ref, bf16[1024,384]{1,0:T(8,128)(2,1)S(1)} %get-tuple-element.38.ff_ref, f32[2,4,64,128]{3,2,1,0:T(8,128)S(1)} %get-tuple-element.39.rows_ref, ...), custom_call_target="tpu_custom_call" | custom-call | tf_op jit(solution)/shard_map/cond/branch_1_fun/finish/pallas_call | solution.py:468
Async XLA Ops:
  0.0 42.0 %copy-start.2 = (bf16[3,960,60]{1,2,0:T(8,128)(2,1)S(1)}, bf16[3,960,60]{1,2,0:T(8,128)(2,1)}, u32[]{:S(2)}) copy-start(bf16[3,960,60]{1,2,0:T(8,128)(2,1)} %param.8) | copy-start | bytes 1036804
  0.0 42.0 %copy-start.3 = (f32[12]{0:T(128)S(1)}, f32[12]{0:T(128)}, u32[]{:S(2)}) copy-start(f32[12]{0:T(128)} %occ_energy_hbm.1) | copy-start | bytes 148
  0.0 42.0 %copy-start.4 = (s32[12]{0:T(128)S(1)}, s32[12]{0:T(128)}, u32[]{:S(2)}) copy-start(s32[12]{0:T(128)} %occ_irrep_hbm.1) | copy-start | bytes 148

commit v6 on v5

--- a/solution.py
+++ b/solution.py
@@ -290,9 +290,9 @@
     for n in range(X):
         assemble(ms.at[pl.ds(ROWS * n, ROWS)], blocks, [brow[n, i3] for i3 in range(PAIRS)], cols)
     sub = lax.broadcasted_iota(I32, (ROWS, WINDOW), 0)
-    for n in range(X):
-        rows = slice(ROWS * n, ROWS * (n + 1))
-        res = jnp.dot(ms[rows], ff_out[...], preferred_element_type=F32)
+    sums = jnp.dot(ms[...], ff_out[...], preferred_element_type=F32)
+    for n in range(X):
+        res = sums[ROWS * n : ROWS * (n + 1)]
         res = jnp.where(sub < ROWS - REM, res, flag_s[0:1, 0:1]).astype(BF16)
         part[0, n] = res[: ROWS // 2]
         part[1, n] = res[ROWS // 2 :]
@@ -439,9 +439,10 @@
 
 
 def finish_kernel(m_ref, inter_ref, ff_ref, rows_ref, cols_ref, out_hbm, out, res, sem):
-    for n in range(X):
-        inter = jnp.concatenate([inter_ref[4 * n + c] for c in range(4)], axis=0)
-        cycle = lax.dot_general(inter, ff_ref[...], (((1,), (1,)), ((), ())), preferred_element_type=F32)
+    inter = inter_ref[...].reshape(X * ROWS, WINDOW)
+    whole = lax.dot_general(inter, ff_ref[...], (((1,), (1,)), ((), ())), preferred_element_type=F32)
+    for n in range(X):
+        cycle = whole[ROWS * n : ROWS * (n + 1)]
         rlab = jnp.concatenate([rows_ref[0, n]] * 2, axis=1)
         ren = jnp.concatenate([rows_ref[1, n]] * 2, axis=1)
         for g in range(GROUPS):

time: 44.2 us -> 43.7 us (0.989)
  Pallas kernels: 43.4 us -> 42.9 us
where the time goes in v6:
time: 43.7 us; the launch traced here: 43.6 us
  Pallas kernels  42.9 us (98%)
  between operations  0.67 us (2%)
    pallas_call x1, Pallas kernels, exchange(): pl.pallas_call(exchange_kernel, out_shape=[pltpu.VMEM(*s) for s in shapes...  41.2 us
    pallas_call x1, Pallas kernels, finish(): pl.pallas_call(finish_kernel, out_shape=pltpu.HBM((OCC, OCC, SLAB, WIDTH)...  1.68 us

profile of v6, /device:TPU:1, one launch (start us, length us, event | category | flops | bytes accessed | tf_op | source)
XLA Modules:
  0.0 43.6 jit_solution(2815632994454973445)
XLA Ops:
  0.0 0.0 copy-start.2
  0.0 0.0 copy-start.3
  0.0 0.0 copy-start.4
  0.0 41.2 %exchange.1 = (bf16[4,64,1024]{2,1,0:T(8,128)(2,1)S(1)}, bf16[16,16,384]{2,1,0:T(8,128)(2,1)S(1)}, bf16[1024,384]{1,0:T(8,128)(2,1)S(1)}, f32[2,4,64,128]{3,2,1,...) custom-call(bf16[3,60,960]{2,1,0:T(8,128)(2,1)} %bitcast.28, bf16[12,60,2048]{2,1,0:T(8,128)(2,1)} %fac_hbm.1, ...), custom_call_target="tpu_custom_call" | custom-call | tf_op jit(solution)/shard_map/exchange/pallas_call | solution.py:405
  41.8 0.0 copy-done.2
  41.8 0.0 copy-done.3
  41.9 0.0 copy-done.4
  41.9 1.7 %conditional.1 = (f32[12,20,12,60]{3,1,2,0:T(8,128)}) conditional(s32[]{:T(128)} %bitcast.13, (s32[12]{0:T(128)S(1)}, s32[960]{0:T(1024)}, bf16[3,960,60]{1,2,0:T(8,128)(2,1)S(1)}, bf16[12,60,2048]{2,1,0:T(8,128)(2,1)}, f32[12]{0:T(128)S(1)}, /*index=5*/f32[960]{0:T(1024)}) %tuple.22, (bf16[4,64,1024]{2,1,0:T(8,128)(2,1)S(1)}, ...), branch_computations={%region_0.2_spmd, %region_2.3_spmd} | conditional | flops 1417743616 | bytes 34242272 | solution.py:487
  41.9 1.7 %finish.1 = f32[12,12,20,60]{3,2,1,0:T(8,128)} custom-call(bf16[4,64,1024]{2,1,0:T(8,128)(2,1)S(1)} %get-tuple-element.36.m_ref, bf16[16,16,384]{2,1,0:T(8,128)(2,1)S(1)} %get-tuple-element.37.inter_ref, bf16[1024,384]{1,0:T(8,128)(2,1)S(1)} %get-tuple-element.38.ff_ref, f32[2,4,64,128]{3,2,1,0:T(8,128)S(1)} %get-tuple-element.39.rows_ref, ...), custom_call_target="tpu_custom_call" | custom-call | tf_op jit(solution)/shard_map/cond/branch_1_fun/finish/pallas_call | solution.py:469
Async XLA Ops:
  0.0 41.8 %copy-start.2 = (bf16[3,960,60]{1,2,0:T(8,128)(2,1)S(1)}, bf16[3,960,60]{1,2,0:T(8,128)(2,1)}, u32[]{:S(2)}) copy-start(bf16[3,960,60]{1,2,0:T(8,128)(2,1)} %param.8) | copy-start | bytes 1036804
  0.0 41.8 %copy-start.3 = (f32[12]{0:T(128)S(1)}, f32[12]{0:T(128)}, u32[]{:S(2)}) copy-start(f32[12]{0:T(128)} %occ_energy_hbm.1) | copy-start | bytes 148
  0.0 41.8 %copy-start.4 = (s32[12]{0:T(128)S(1)}, s32[12]{0:T(128)}, u32[]{:S(2)}) copy-start(s32[12]{0:T(128)} %occ_irrep_hbm.1) | copy-start | bytes 148

commit v7 on v6

--- a/solution.py
+++ b/solution.py
@@ -404,7 +404,7 @@
     dma = pltpu.SemaphoreType.DMA
     return pl.pallas_call(
         exchange_kernel,
-        out_shape=[pltpu.VMEM(*s) for s in shapes] + [jax.ShapeDtypeStruct((1,), F32)],
+        out_shape=[pltpu.VMEM(*s) for s in shapes] + [pltpu.SMEM((1,), F32)],
         in_specs=[hbm] * 6,
         out_specs=[pl.BlockSpec(memory_space=pltpu.VMEM)] * 5 + [smem],
         scratch_shapes=[

time: 43.7 us -> 42.5 us (0.973)
  between operations: 0.67 us -> 0.04 us
  Pallas kernels: 42.9 us -> 42.3 us
    pallas_call x1, Pallas kernels: 41.2 us -> 40.7 us  [exchange(): pl.pallas_call(exchange_kernel, out_shape=[pltpu.VMEM(*s) for s in shapes...]
where the time goes in v7:
time: 42.5 us; the launch traced here: 42.4 us
  Pallas kernels  42.3 us (100%)
    pallas_call x1, Pallas kernels, exchange(): pl.pallas_call(exchange_kernel, out_shape=[pltpu.VMEM(*s) for s in shapes...  40.7 us
    pallas_call x1, Pallas kernels, finish(): pl.pallas_call(finish_kernel, out_shape=pltpu.HBM((OCC, OCC, SLAB, WIDTH)...  1.68 us

profile of v7, /device:TPU:1, one launch (start us, length us, event | category | flops | bytes accessed | tf_op | source)
XLA Modules:
  0.0 42.4 jit_solution(8402081310989484374)
XLA Ops:
  0.0 0.0 copy-start.2
  0.0 0.0 copy-start.3
  0.0 0.0 copy-start.4
  0.0 40.7 %exchange.1 = (bf16[4,64,1024]{2,1,0:T(8,128)(2,1)S(1)}, bf16[16,16,384]{2,1,0:T(8,128)(2,1)S(1)}, bf16[1024,384]{1,0:T(8,128)(2,1)S(1)}, f32[2,4,64,128]{3,2,1,...) custom-call(bf16[3,60,960]{2,1,0:T(8,128)(2,1)} %bitcast.28, bf16[12,60,2048]{2,1,0:T(8,128)(2,1)} %fac_hbm.1, ...), custom_call_target="tpu_custom_call" | custom-call | tf_op jit(solution)/shard_map/exchange/pallas_call | solution.py:405
  40.7 0.0 copy-done.2
  40.7 0.0 copy-done.3
  40.7 0.0 copy-done.4
  40.7 1.7 %conditional.1 = (f32[12,20,12,60]{3,1,2,0:T(8,128)}) conditional(s32[]{:T(128)} %bitcast.13, (s32[12]{0:T(128)S(1)}, s32[960]{0:T(1024)}, bf16[3,960,60]{1,2,0:T(8,128)(2,1)S(1)}, bf16[12,60,2048]{2,1,0:T(8,128)(2,1)}, f32[12]{0:T(128)S(1)}, /*index=5*/f32[960]{0:T(1024)}) %tuple.22, (bf16[4,64,1024]{2,1,0:T(8,128)(2,1)S(1)}, ...), branch_computations={%region_0.2_spmd, %region_2.3_spmd} | conditional | flops 1417743616 | bytes 34242272 | solution.py:487
  40.7 1.7 %finish.1 = f32[12,12,20,60]{3,2,1,0:T(8,128)} custom-call(bf16[4,64,1024]{2,1,0:T(8,128)(2,1)S(1)} %get-tuple-element.36.m_ref, bf16[16,16,384]{2,1,0:T(8,128)(2,1)S(1)} %get-tuple-element.37.inter_ref, bf16[1024,384]{1,0:T(8,128)(2,1)S(1)} %get-tuple-element.38.ff_ref, f32[2,4,64,128]{3,2,1,0:T(8,128)S(1)} %get-tuple-element.39.rows_ref, ...), custom_call_target="tpu_custom_call" | custom-call | tf_op jit(solution)/shard_map/cond/branch_1_fun/finish/pallas_call | solution.py:469
Async XLA Ops:
  0.0 40.7 %copy-start.2 = (bf16[3,960,60]{1,2,0:T(8,128)(2,1)S(1)}, bf16[3,960,60]{1,2,0:T(8,128)(2,1)}, u32[]{:S(2)}) copy-start(bf16[3,960,60]{1,2,0:T(8,128)(2,1)} %param.8) | copy-start | bytes 1036804
  0.0 40.7 %copy-start.3 = (f32[12]{0:T(128)S(1)}, f32[12]{0:T(128)}, u32[]{:S(2)}) copy-start(f32[12]{0:T(128)} %occ_energy_hbm.1) | copy-start | bytes 148
  0.0 40.7 %copy-start.4 = (s32[12]{0:T(128)S(1)}, s32[12]{0:T(128)}, u32[]{:S(2)}) copy-start(s32[12]{0:T(128)} %occ_irrep_hbm.1) | copy-start | bytes 148

commit v8 on v7

--- a/solution.py
+++ b/solution.py
@@ -307,7 +307,8 @@
         send[n, 0] = total[:MAIN]
         send[n, 1] = total[MAIN:]
 
-    for n in range(X):
+    for d in (2, 1, 3, 0):
+        n = (x + d) % X
         for h in range(2):
             to = reducer(n, h)
 

time: 42.5 us -> 42.9 us (level)
  no operation moved by 1% of the time
where the time goes in v8:
time: 42.9 us; the launch traced here: 42.8 us
  Pallas kernels  42.7 us (100%)
    pallas_call x1, Pallas kernels, exchange(): pl.pallas_call(exchange_kernel, out_shape=[pltpu.VMEM(*s) for s in shapes...  41.1 us
    pallas_call x1, Pallas kernels, finish(): pl.pallas_call(finish_kernel, out_shape=pltpu.HBM((OCC, OCC, SLAB, WIDTH)...  1.68 us

profile of v8, /device:TPU:1, one launch (start us, length us, event | category | flops | bytes accessed | tf_op | source)
XLA Modules:
  0.0 42.8 jit_solution(15805730535390506088)
XLA Ops:
  0.0 0.0 copy-start.2
  0.0 0.0 copy-start.3
  0.0 0.0 copy-start.4
  0.0 41.1 %exchange.1 = (bf16[4,64,1024]{2,1,0:T(8,128)(2,1)S(1)}, bf16[16,16,384]{2,1,0:T(8,128)(2,1)S(1)}, bf16[1024,384]{1,0:T(8,128)(2,1)S(1)}, f32[2,4,64,128]{3,2,1,...) custom-call(bf16[3,60,960]{2,1,0:T(8,128)(2,1)} %bitcast.28, bf16[12,60,2048]{2,1,0:T(8,128)(2,1)} %fac_hbm.1, ...), custom_call_target="tpu_custom_call" | custom-call | tf_op jit(solution)/shard_map/exchange/pallas_call | solution.py:406
  41.1 0.0 copy-done.2
  41.1 0.0 copy-done.3
  41.1 0.0 copy-done.4
  41.1 1.7 %conditional.1 = (f32[12,20,12,60]{3,1,2,0:T(8,128)}) conditional(s32[]{:T(128)} %bitcast.13, (s32[12]{0:T(128)S(1)}, s32[960]{0:T(1024)}, bf16[3,960,60]{1,2,0:T(8,128)(2,1)S(1)}, bf16[12,60,2048]{2,1,0:T(8,128)(2,1)}, f32[12]{0:T(128)S(1)}, /*index=5*/f32[960]{0:T(1024)}) %tuple.22, (bf16[4,64,1024]{2,1,0:T(8,128)(2,1)S(1)}, ...), branch_computations={%region_0.2_spmd, %region_2.3_spmd} | conditional | flops 1417743616 | bytes 34242272 | solution.py:488
  41.1 1.7 %finish.1 = f32[12,12,20,60]{3,2,1,0:T(8,128)} custom-call(bf16[4,64,1024]{2,1,0:T(8,128)(2,1)S(1)} %get-tuple-element.36.m_ref, bf16[16,16,384]{2,1,0:T(8,128)(2,1)S(1)} %get-tuple-element.37.inter_ref, bf16[1024,384]{1,0:T(8,128)(2,1)S(1)} %get-tuple-element.38.ff_ref, f32[2,4,64,128]{3,2,1,0:T(8,128)S(1)} %get-tuple-element.39.rows_ref, ...), custom_call_target="tpu_custom_call" | custom-call | tf_op jit(solution)/shard_map/cond/branch_1_fun/finish/pallas_call | solution.py:470
Async XLA Ops:
  0.0 41.1 %copy-start.2 = (bf16[3,960,60]{1,2,0:T(8,128)(2,1)S(1)}, bf16[3,960,60]{1,2,0:T(8,128)(2,1)}, u32[]{:S(2)}) copy-start(bf16[3,960,60]{1,2,0:T(8,128)(2,1)} %param.8) | copy-start | bytes 1036804
  0.0 41.1 %copy-start.3 = (f32[12]{0:T(128)S(1)}, f32[12]{0:T(128)}, u32[]{:S(2)}) copy-start(f32[12]{0:T(128)} %occ_energy_hbm.1) | copy-start | bytes 148
  0.0 41.1 %copy-start.4 = (s32[12]{0:T(128)S(1)}, s32[12]{0:T(128)}, u32[]{:S(2)}) copy-start(s32[12]{0:T(128)} %occ_irrep_hbm.1) | copy-start | bytes 148
